TPU v7x, 32 devices: a whole 2x2x4 slice. The times are simulated.
32 devices in a mesh: span: 16 (over z, y, x), width: 2 (over core).
Axes of the slice: x: 2, y: 2, z: 4, core: 2. Of those that a mesh axis runs over, the one named last changes fastest.
Arguments:
- state: float32 [4, 128, 64, 128], P(None, 'span', 'width'), may hold values from 0.2 to 2
- source: float32 [4, 128, 64, 128], P(None, 'span', 'width'), may hold values from -6 to 8
- conductance: float32 [128, 64, 128], P('span', 'width'), may hold values from 0.5 to 2
- rebar_cover: int32 [128, 64, 128], P('span', 'width'), may hold values 0 or 1
- colour: int32 [16, 2], P('span', 'width'), may hold values from 0 to 1
- diffusivity: float32 [4], replicated, may hold values from 0.5 to 2
- binding: float32 [4], replicated, may hold values from 0.1 to 1
Outputs:
- updated: float32 [4, 128, 64, 128], P(None, 'span', 'width')
- residual: float32 [4, 128, 64, 128], P(None, 'span', 'width')
All inputs are finite; a program needn't handle non-finite values. No bound on the sum of `rebar_cover` on one device may be relied on, other than what follows from the above.
Results may differ from a plain program's by a relative error of at most 0.002.
Values sent between devices are 32-bit elements; how exact they have to be, the bound alone decides.
A program may use at most 64 MiB of HBM per device.

v0:
```python
import functools

import jax
import jax.numpy as jnp
from jax import lax
from jax.experimental import pallas as pl
from jax.experimental.pallas import tpu as pltpu
from jax.sharding import PartitionSpec as P

COARSEN = 8
SWEEPS = 4
COARSE_ITERS = 20
INV_STEP = 0.05
EPSILON = 1e-06
MESH = pl.DeviceIdType.MESH
F32 = jnp.float32


def kernel(
    n_span, n_width, ions, cx, cy, cz,
    state_hbm, source_hbm, cond_hbm, cover_hbm, colour_ref, spread_ref, strength_ref,
    up_ref, res_ref,
    state_ref, source_ref, cond_ref, cover_ref, xs, xh, ys, yh, first, gath, part, condp, coverp, rhs, diag, c, a, d, image,
    mx, fx, cx_sum, aj, cj, ej, sp, wv,
    send_sem, recv_sem, gsend, grecv, psend, precv, in_sem, met,
):
    s = lax.axis_index("span")
    w = lax.axis_index("width")
    kp = cx // 2
    rows = cy // COARSEN
    row = lax.broadcasted_iota(jnp.int32, (cy, cz), 0)
    lane = lax.broadcasted_iota(jnp.int32, (cy, cz), 1)
    p = (row + lane) % 2 == 1
    first_y, last_y = row == 0, row == cy - 1
    first_z, last_z = lane == 0, lane == cz - 1

    loads = [
        pltpu.make_async_copy(src, dst, in_sem.at[k])
        for k, (src, dst) in enumerate((
            (state_hbm, state_ref), (cond_hbm, cond_ref),
            (cover_hbm, cover_ref), (source_hbm, source_ref)))
    ]
    for load in loads:
        load.start()

    barrier = pltpu.get_barrier_semaphore()

    has = (s < n_span - 1, s > 0, w < n_width - 1, w > 0)
    gets = (s > 0, s < n_span - 1, w > 0, w < n_width - 1)
    to = ((s + 1, w), (s - 1, w), (s, w + 1), (s, w - 1))

    def flip(v, bit):
        return v + bit - 2 * bit * (v // bit % 2)

    bits = [1 << k for k in range((max(n_span, n_width) - 1).bit_length())]
    hops = [(s, flip(w, b)) for b in bits if b < n_width]
    hops += [(flip(s, b), w) for b in bits if b < n_span]
    far = [(s, flip(w, b)) for b in bits if 1 < b < n_width]
    far += [(flip(s, b), w) for b in bits if 1 < b < n_span]
    for k in range(4):
        @pl.when(has[k])
        def _():
            pl.semaphore_signal(barrier, inc=1, device_id=to[k], device_id_type=MESH)
    for other in far:
        pl.semaphore_signal(barrier, inc=1, device_id=other, device_id_type=MESH)

    def meet(which):
        for k in which:
            if 0 <= k < len(hops):
                pl.semaphore_signal(
                    met.at[k], inc=1, device_id=hops[k], device_id_type=MESH)

    def met_by(which):
        for k in which:
            if 0 <= k < len(hops):
                pl.semaphore_wait(met.at[k], 1)

    def split(x):
        pairs = x.reshape(kp, 2, cy, cz)
        even, odd = pairs[:, 0], pairs[:, 1]
        return jnp.where(p, odd, even), jnp.where(p, even, odd)

    def yz_sum(v):
        out = jnp.where(last_y, 0.0, pltpu.roll(v, cy - 1, v.ndim - 2))
        out += jnp.where(first_y, 0.0, pltpu.roll(v, 1, v.ndim - 2))
        out += jnp.where(last_z, 0.0, pltpu.roll(v, cz - 1, v.ndim - 1))
        out += jnp.where(first_z, 0.0, pltpu.roll(v, 1, v.ndim - 1))
        return out

    zero_face = jnp.zeros((1, cy, cz), F32)

    def nb_red(black):
        above = jnp.concatenate([black[1:], zero_face], axis=0)
        below = jnp.concatenate([zero_face, black[:-1]], axis=0)
        return black + jnp.where(p, above, below) + yz_sum(black)

    def nb_black(red):
        above = jnp.concatenate([red[1:], zero_face], axis=0)
        below = jnp.concatenate([zero_face, red[:-1]], axis=0)
        return red + jnp.where(p, below, above) + yz_sum(red)

    def rim(e, i):
        lo, hi = xh[e, 0, i], xh[e, 1, i]
        ylo, yhi = yh[e, 0, i], yh[e, 1, i]
        mid = jnp.zeros((kp - 2, cy, cz), F32)

        def faces(k0, k1, half):
            x_part = jnp.concatenate([k0[None], mid, k1[None]], axis=0)
            low = ylo[half * kp:(half + 1) * kp][:, None, :]
            high = yhi[half * kp:(half + 1) * kp][:, None, :]
            return x_part + jnp.where(first_y, low, 0.0) + jnp.where(last_y, high, 0.0)

        red = faces(jnp.where(p, 0.0, lo), jnp.where(p, hi, 0.0), 1)
        black = faces(jnp.where(p, lo, 0.0), jnp.where(p, 0.0, hi), 0)
        return red, black

    def put_y(e, i, red, black):
        ys[e, 0, i] = jnp.concatenate([red[:, cy - 1, :], black[:, cy - 1, :]], axis=0)
        ys[e, 1, i] = jnp.concatenate([red[:, 0, :], black[:, 0, :]], axis=0)

    def put_x(e, i, red, black):
        xs[e - 1, 0, i] = jnp.where(p, red[kp - 1], black[kp - 1])
        xs[e - 1, 1, i] = jnp.where(p, black[0], red[0])

    pair_of = ions // 2

    def copy(e, k, g):
        own = pl.ds(g * pair_of, pair_of)
        if k >= 2:
            src, dst = ys.at[e, k - 2, own], yh.at[e, k - 2, own]
        else:
            dst = xh.at[e, k, own]
            if e == 0:
                src = state_ref.at[own, cx - 1] if k == 0 else state_ref.at[own, 0]
            else:
                src = xs.at[e - 1, k, own]
        return pltpu.make_async_remote_copy(
            src_ref=src, dst_ref=dst, send_sem=send_sem.at[e, k, g], recv_sem=recv_sem.at[e, k, g],
            device_id=to[k], device_id_type=MESH,
        )

    def send(e, g):
        for k in range(4):
            @pl.when(has[k])
            def _():
                copy(e, k, g).start()

    def receive(e, g):
        for k in range(4):
            @pl.when(gets[k])
            def _():
                copy(e, k, g).wait_recv()

    for k in range(4):
        @pl.when(jnp.logical_not(gets[k]))
        def _():
            for e in range(3):
                if k >= 2:
                    yh[e, k - 2] = jnp.zeros(yh.shape[2:], F32)
                else:
                    xh[e, k] = jnp.zeros(xh.shape[2:], F32)

    def pack_state(i, _):
        put_y(0, i, *split(state_ref[i]))
        return 0

    loads[0].wait()
    lax.fori_loop(0, ions, pack_state, 0)
    near = sum(g.astype(jnp.int32) for g in gets)
    pl.semaphore_wait(barrier, near + len(far))
    send(0, 0)
    send(0, 1)
    meet((0,))

    for load in loads[1:]:
        load.wait()
    condp[0], condp[1] = split(cond_ref[...])
    coverp[0], coverp[1] = split(cover_ref[...].astype(F32))
    cx_sum[...] = jnp.sum(cond_ref[...], axis=0)

    def local_terms(i, _):
        spread, strength = spread_ref[i], strength_ref[i]
        st = split(state_ref[i])
        src = split(source_ref[i])
        near = (nb_red(st[1]), nb_black(st[0]))
        mass_sum = jnp.zeros((cy, cz), F32)
        for h in range(2):
            coef = spread * condp[h]
            inv = 1.0 / (1.0 + st[h])
            bound = coverp[h] * strength * inv
            mass = INV_STEP + bound * inv
            dg = mass + 6.0 * coef
            diag[h, i] = dg
            c[h, i] = coef / dg
            rhs[h, i] = src[h] - (coef * (6.0 * st[h] - near[h]) + bound * st[h])
            mass_sum += jnp.sum(mass, axis=0)
        mx[i] = mass_sum
        return 0

    lax.fori_loop(0, ions, local_terms, 0)
    met_by((0,))
    meet((1,))

    mine = colour_ref[0, 0].astype(F32)

    def sweeps(ar, ab, cr, cb):
        red = ar
        black = ab + cb * nb_black(red)
        for _ in range(SWEEPS - 1):
            red = ar + cr * nb_red(black)
            black = ab + cb * nb_black(red)
        return red, black

    def phase_zero(i, _):
        near = rim(0, i)
        for h in range(2):
            right = rhs[h, i] + spread_ref[i] * condp[h] * near[h]
            rhs[h, i] = right
            a[h, i] = right / diag[h, i]
        red, black = sweeps(
            (1.0 - mine) * a[0, i], (1.0 - mine) * a[1, i], c[0, i], c[1, i]
        )
        d[0, i], d[1, i] = red, black
        put_y(1, i, red, black)
        put_x(1, i, red, black)
        return 0

    def halves(e, body):
        for g in range(2):
            receive(e, g)
            lax.fori_loop(g * pair_of, (g + 1) * pair_of, body, 0, unroll=2)
            if e < 2:
                send(e + 1, g)

    halves(0, phase_zero)
    met_by((1,))
    meet((2,))
    met_by((2,))
    meet((3,))

    def phase_one(i, _):
        near = rim(1, i)
        red, black = sweeps(
            mine * (a[0, i] + c[0, i] * near[0]), mine * (a[1, i] + c[1, i] * near[1]),
            c[0, i], c[1, i],
        )
        red, black = red + d[0, i], black + d[1, i]
        d[0, i], d[1, i] = red, black
        put_y(2, i, red, black)
        put_x(2, i, red, black)
        return 0

    halves(1, phase_one)
    met_by((3,))
    meet((4,))

    eighth = lane % COARSEN

    def coarse_pack(parts):
        acc = jnp.zeros((cy, cz), F32)
        for i in range(ions):
            v = parts[i]
            for step in (1, 2, 4):
                v = v + pltpu.roll(v, cz - step, 1)
            if i:
                v = pltpu.roll(v, i, 1)
            acc = jnp.where(eighth == i, v, acc)
        return jnp.concatenate(
            [jnp.sum(acc[j * COARSEN:(j + 1) * COARSEN], axis=0, keepdims=True)
             for j in range(rows)], axis=0)

    cond_sum = cx_sum[...]
    coarse_off = coarse_pack([spread_ref[i] * cond_sum for i in range(ions)]) / COARSEN
    coarse_diag = coarse_pack([mx[i] for i in range(ions)]) + 6.0 * coarse_off
    coarse_inv = 1.0 / jnp.where(eighth[:rows] < ions, coarse_diag, 1.0)


    def fine_terms(i, _):
        near = rim(2, i)
        red, black = d[0, i], d[1, i]
        near = (near[0] + nb_red(black), near[1] + nb_black(red))
        total = jnp.zeros((cy, cz), F32)
        for h, v in ((0, red), (1, black)):
            fine = rhs[h, i] - (diag[h, i] * v - spread_ref[i] * condp[h] * near[h])
            rhs[h, i] = fine
            total += jnp.sum(fine, axis=0)
        fx[i] = total
        return 0

    met_by((4,))
    for k in range(5, len(hops)):
        meet((k,))
        met_by((k,))
    halves(2, fine_terms)
    crhs = coarse_pack([fx[i] for i in range(ions)])
    first[w] = jnp.concatenate([crhs * coarse_inv, coarse_off * coarse_inv], axis=0)

    def to_row(buf, ssem, rsem):
        for off in range(1, n_width):
            pltpu.make_async_remote_copy(
                src_ref=buf.at[w], dst_ref=buf.at[w], send_sem=ssem, recv_sem=rsem,
                device_id=(s, lax.rem(w + off, n_width)), device_id_type=MESH,
            ).start()

    def to_column(buf, ssem, rsem):
        @pl.loop(1, n_span)
        def _(off):
            pltpu.make_async_remote_copy(
                src_ref=buf.at[s], dst_ref=buf.at[s], send_sem=ssem, recv_sem=rsem,
                device_id=(lax.rem(s + off, n_span), w), device_id_type=MESH,
            ).start()

    def all_of(buf, sem, count):
        others = buf.at[pl.ds(0, count - 1)]
        pltpu.make_async_copy(others, others, sem).wait()

    to_row(first, gsend.at[0], grecv.at[0])
    all_of(first, grecv.at[0], n_width)
    gath[s] = first[...]
    to_column(gath, gsend.at[1], grecv.at[1])
    all_of(gath, grecv.at[1], n_span)

    wide = n_width * rows
    g = gath[...]
    aj[...] = jnp.concatenate([g[:, k, :rows] for k in range(n_width)], axis=1)
    cj[...] = jnp.concatenate([g[:, k, rows:] for k in range(n_width)], axis=1)
    crow = lax.broadcasted_iota(jnp.int32, (wide, cz), 0)
    clane = lax.broadcasted_iota(jnp.int32, (wide, cz), 1)
    zero_c = jnp.zeros((1, wide, cz), F32)

    def jacobi(_, e):
        total = jnp.concatenate([e[1:], zero_c], axis=0)
        total += jnp.concatenate([zero_c, e[:-1]], axis=0)
        total += jnp.where(crow == wide - 1, 0.0, pltpu.roll(e, wide - 1, 1))
        total += jnp.where(crow == 0, 0.0, pltpu.roll(e, 1, 1))
        total += jnp.where(clane >= cz - COARSEN, 0.0, pltpu.roll(e, cz - COARSEN, 2))
        total += jnp.where(clane < COARSEN, 0.0, pltpu.roll(e, COARSEN, 2))
        return aj[...] + cj[...] * total

    e = lax.fori_loop(0, COARSE_ITERS - 1, jacobi, aj[...])
    ej[0] = zero_c[0]
    ej[n_span + 1] = zero_c[0]
    ej[1:n_span + 1] = e
    before, here, after = ej[s], ej[s + 1], ej[s + 2]

    def own_rows(v):
        out = v[:rows]
        for k in range(1, n_width):
            out = jnp.where(w == k, v[k * rows:(k + 1) * rows], out)
        return out

    y_low = jnp.zeros((1, cz), F32)
    y_high = jnp.zeros((1, cz), F32)
    for k in range(n_width):
        if k > 0:
            y_low = jnp.where(w == k, here[k * rows - 1:k * rows], y_low)
        if k < n_width - 1:
            y_high = jnp.where(w == k, here[(k + 1) * rows:(k + 1) * rows + 1], y_high)
    packed = jnp.concatenate(
        [own_rows(here), own_rows(before), own_rows(after), y_low, y_high,
         jnp.zeros((16 - 3 * rows - 2, cz), F32)], axis=0)
    for i in range(ions):
        v = jnp.where(eighth[:16] == i, packed, 0.0)
        if i:
            v = pltpu.roll(v, cz - i, 1)
        for step in (1, 2, 4):
            v = v + pltpu.roll(v, step, 1)
        sp[i] = v

    def tall(v):
        return jnp.concatenate(
            [jnp.broadcast_to(v[j:j + 1], (COARSEN, cz)) for j in range(rows)], axis=0)

    sums = []
    for i in range(ions):
        v = sp[i]
        lift = tall(v[:rows])
        lo, hi = tall(v[rows:2 * rows]), tall(v[2 * rows:3 * rows])
        base = yz_sum(lift) + lift
        base += jnp.where(first_y, v[3 * rows:3 * rows + 1], 0.0)
        base += jnp.where(last_y, v[3 * rows + 1:3 * rows + 2], 0.0)
        numer = jnp.zeros((cy, cz), F32)
        denom = jnp.zeros((cy, cz), F32)
        for h in range(2):
            for k in range(kp):
                side = lift
                low_side = p if h else jnp.logical_not(p)
                high_side = jnp.logical_not(p) if h else p
                if k == 0:
                    side = jnp.where(low_side, lo, side)
                if k == kp - 1:
                    side = jnp.where(high_side, hi, side)
                im = diag[h, i, k] * lift - spread_ref[i] * condp[h, k] * (base + side)
                image[h, i, k] = im
                numer += rhs[h, i, k] * im
                denom += im * im
        sums.append((jnp.sum(numer, axis=0, keepdims=True), jnp.sum(denom, axis=0, keepdims=True)))
    me = s * n_width + w
    part[me] = jnp.concatenate([n for n, _ in sums] + [m for _, m in sums], axis=0)
    everyone = n_span * n_width

    @pl.loop(1, everyone)
    def _(off):
        other = lax.rem(me + off, everyone)
        pltpu.make_async_remote_copy(
            src_ref=part.at[me], dst_ref=part.at[me], send_sem=psend, recv_sem=precv,
            device_id=(other // n_width, other % n_width), device_id_type=MESH,
        ).start()

    all_of(part, precv, everyone)
    whole = jnp.sum(jnp.sum(part[...], axis=0), axis=1, keepdims=True)
    weight = whole[:ions] / (whole[ions:] + EPSILON)
    wv[...] = jnp.broadcast_to(weight, (ions, cz))

    for i in range(ions):
        wt = wv[i:i + 1]
        lifted = wt * tall(sp[i, :rows])
        for k in range(kp):
            red, black = d[0, i, k], d[1, i, k]
            up_ref[i, 2 * k] = state_ref[i, 2 * k] + (jnp.where(p, black, red) + lifted)
            up_ref[i, 2 * k + 1] = state_ref[i, 2 * k + 1] + (jnp.where(p, red, black) + lifted)
            red = rhs[0, i, k] - wt * image[0, i, k]
            black = rhs[1, i, k] - wt * image[1, i, k]
            res_ref[i, 2 * k] = jnp.where(p, black, red)
            res_ref[i, 2 * k + 1] = jnp.where(p, red, black)

    for e in range(3):
        for k in range(4):
            @pl.when(has[k])
            def _():
                copy(e, k, 0).wait_send()
                copy(e, k, 1).wait_send()
    all_of(first, gsend.at[0], n_width)
    all_of(gath, gsend.at[1], n_span)
    all_of(part, psend, everyone)


def on_device(n_span, n_width, state, source, conductance, rebar_cover, colour, diffusivity, binding):
    ions, cx, cy, cz = state.shape
    kp = cx // 2
    rows = cy // COARSEN
    half = pltpu.VMEM((2, ions, kp, cy, cz), F32)
    pair = pltpu.VMEM((2, kp, cy, cz), F32)
    vmem = pl.BlockSpec(memory_space=pltpu.VMEM)
    smem = pl.BlockSpec(memory_space=pltpu.SMEM)
    dma = pltpu.SemaphoreType.DMA
    return pl.pallas_call(
        functools.partial(kernel, n_span, n_width, ions, cx, cy, cz),
        out_shape=(jax.ShapeDtypeStruct(state.shape, F32),) * 2,
        in_specs=[pl.BlockSpec(memory_space=pltpu.HBM)] * 4 + [smem] * 3,
        out_specs=(vmem, vmem),
        scratch_shapes=[
            pltpu.VMEM(state.shape, F32), pltpu.VMEM(state.shape, F32),
            pltpu.VMEM(conductance.shape, F32), pltpu.VMEM(conductance.shape, jnp.int32),
            pltpu.VMEM((2, 2, ions, cy, cz), F32),
            pltpu.VMEM((3, 2, ions, cy, cz), F32),
            pltpu.VMEM((3, 2, ions, 2 * kp, cz), F32),
            pltpu.VMEM((3, 2, ions, 2 * kp, cz), F32),
            pltpu.VMEM((n_width, 2 * rows, cz), F32),
            pltpu.VMEM((n_span, n_width, 2 * rows, cz), F32),
            pltpu.VMEM((n_span * n_width, 2 * ions, cz), F32),
            pair, pair, half, half, half, half, half, half,
            pltpu.VMEM((ions, cy, cz), F32),
            pltpu.VMEM((ions, cy, cz), F32),
            pltpu.VMEM((cy, cz), F32),
            pltpu.VMEM((n_span, n_width * rows, cz), F32),
            pltpu.VMEM((n_span, n_width * rows, cz), F32),
            pltpu.VMEM((n_span + 2, n_width * rows, cz), F32),
            pltpu.VMEM((ions, 16, cz), F32),
            pltpu.VMEM((ions, cz), F32),
            dma((3, 4, 2)), dma((3, 4, 2)), dma((2,)), dma((2,)), dma, dma, dma((4,)), pltpu.SemaphoreType.REGULAR((max(5, (n_span - 1).bit_length() + (n_width - 1).bit_length()),)),
        ],
        compiler_params=pltpu.CompilerParams(
            collective_id=0, has_side_effects=True, vmem_limit_bytes=60 * 1024 * 1024
        ),
    )(state, source, conductance, rebar_cover, colour, diffusivity, binding)


def solution(mesh):
    in_specs = (
        P(None, "span", "width", None),
        P(None, "span", "width", None),
        P("span", "width", None),
        P("span", "width", None),
        P("span", "width"),
        P(),
        P(),
    )
    out_specs = (P(None, "span", "width", None), P(None, "span", "width", None))
    return jax.shard_map(
        functools.partial(on_device, mesh.shape["span"], mesh.shape["width"]),
        mesh=mesh, in_specs=in_specs, out_specs=out_specs, check_vma=False,
    )
```

profile of v0, /device:TPU:0, one launch (start us, length us, event | category | flops | bytes accessed | tf_op | source)
XLA Modules:
  0.0 39.5 jit_solution(11173694350150328114)
XLA Ops:
  1.3 35.5 %shard_map.86 = (f32[4,8,32,128]{3,2,1,0:T(8,128)}, f32[4,8,32,128]{3,2,1,0:T(8,128)}) custom-call(f32[4,8,32,128]{3,2,1,0:T(8,128)} %state_hbm.1, f32[4,8,32,128]{3,2,1,0:T(8,128)} %source_hbm.1, f32[8,32,128]{2,1,0:T(8,128)} %cond_hbm.1, s32[8,32,128]{2,1,0:T(8,128)} %cover_hbm.1, s32[1,1]{1,0:T(1,128)S(6)} %copy.11.colour_ref, f32[4]{0:T(128)} %spread_ref.1, ...), custom_call_target="tpu_custom_call" | custom-call | tf_op jit(solution)/shard_map/pallas_call | solution.py:447
  36.8 0.0 copy-start
  36.8 1.9 %copy.12 = f32[4,8,32,128]{3,2,1,0:T(8,128)} copy(f32[4,8,32,128]{3,2,1,0:T(8,128)} %get-tuple-element.4) | data formatting | bytes 1048576
  38.7 0.0 copy-done
  38.7 0.8 %copy.13 = f32[4,8,32,128]{3,2,1,0:T(8,128)} copy(f32[4,8,32,128]{3,2,1,0:T(8,128)S(1)} %copy-done) | data formatting | bytes 1048576
Async XLA Ops:
  36.8 1.9 %copy-start = (f32[4,8,32,128]{3,2,1,0:T(8,128)S(1)}, f32[4,8,32,128]{3,2,1,0:T(8,128)}, u32[]{:S(2)}) copy-start(f32[4,8,32,128]{3,2,1,0:T(8,128)} %get-tuple-element.5) | copy-start | bytes 1572868
where the time goes:
time: 39.7 us; the launch traced here: 39.5 us
  Pallas kernels  35.5 us (89%)
  local copies, waits for them, and re-layouts  2.72 us (7%)
  between operations  1.29 us (3%)
    pallas_call x1, Pallas kernels, on_device(): pl.pallas_call(functools.partial(kernel, n_span, n_width, ions, cx, cy, c...  35.5 us
    unnamed x4, local copies, waits for them, and re-layouts  2.72 us

commit v1 on v0

--- a/solution.py
+++ b/solution.py
@@ -13,6 +13,8 @@
 INV_STEP = 0.05
 EPSILON = 1e-06
 MESH = pl.DeviceIdType.MESH
+GROUPS = 2
+UNROLL = 2
 F32 = jnp.float32
 
 
@@ -20,9 +22,9 @@
     n_span, n_width, ions, cx, cy, cz,
     state_hbm, source_hbm, cond_hbm, cover_hbm, colour_ref, spread_ref, strength_ref,
     up_ref, res_ref,
-    state_ref, source_ref, cond_ref, cover_ref, xs, xh, ys, yh, first, gath, part, condp, coverp, rhs, diag, c, a, d, image,
-    mx, fx, cx_sum, aj, cj, ej, sp, wv,
-    send_sem, recv_sem, gsend, grecv, psend, precv, in_sem, met,
+    state_ref, source_ref, cond_ref, cover_ref, xs, xh, ys, yh, ysc, xhc, yhc, ops, gath, part, condp, coverp, rhs, diag, c, a, d, image,
+    mx, fx, py, aj, cj, ej, sp, wv,
+    send_sem, recv_sem, csend, crecv, osend, orecv, gsend, grecv, psend, precv, in_sem, met,
 ):
     s = lax.axis_index("span")
     w = lax.axis_index("width")
@@ -52,28 +54,47 @@
     def flip(v, bit):
         return v + bit - 2 * bit * (v // bit % 2)
 
-    bits = [1 << k for k in range((max(n_span, n_width) - 1).bit_length())]
-    hops = [(s, flip(w, b)) for b in bits if b < n_width]
-    hops += [(flip(s, b), w) for b in bits if b < n_span]
-    far = [(s, flip(w, b)) for b in bits if 1 < b < n_width]
-    far += [(flip(s, b), w) for b in bits if 1 < b < n_span]
-    for k in range(4):
-        @pl.when(has[k])
+    quad = 4
+    high = [1 << k for k in range(2, (n_span - 1).bit_length())]
+    partners = [lax.rem(w + k, n_width) for k in range(1, n_width)]
+    quads = [s - s % quad + (s + k) % quad for k in range(1, quad)]
+    greet = [(s, v) for v in partners] + [(t, w) for t in quads] + [(flip(s, b), w) for b in high]
+    up_far = (s % quad == quad - 1) & (s < n_span - 1)
+    down_far = (s % quad == 0) & (s > 0)
+    rounds = [
+        [(s, v) for v in partners] + [(t, w) for t in quads],
+        [(flip(s, high[0]), w)] + [(flip(s, b), v) for b in high[:2] for v in partners],
+    ] + [[(flip(s, b), w)] for b in high[2:]]
+    for other in greet:
+        pl.semaphore_signal(barrier, inc=1, device_id=other, device_id_type=MESH)
+    for ok, other in ((up_far, (s + 1, w)), (down_far, (s - 1, w))):
+        @pl.when(ok)
         def _():
-            pl.semaphore_signal(barrier, inc=1, device_id=to[k], device_id_type=MESH)
-    for other in far:
-        pl.semaphore_signal(barrier, inc=1, device_id=other, device_id_type=MESH)
-
-    def meet(which):
-        for k in which:
-            if 0 <= k < len(hops):
-                pl.semaphore_signal(
-                    met.at[k], inc=1, device_id=hops[k], device_id_type=MESH)
-
-    def met_by(which):
-        for k in which:
-            if 0 <= k < len(hops):
-                pl.semaphore_wait(met.at[k], 1)
+            pl.semaphore_signal(barrier, inc=1, device_id=other, device_id_type=MESH)
+    greeted = len(greet) + up_far.astype(jnp.int32) + down_far.astype(jnp.int32)
+
+    def meet(k):
+        for other in rounds[k]:
+            pl.semaphore_signal(met.at[k], inc=1, device_id=other, device_id_type=MESH)
+
+    def met_by(k):
+        pl.semaphore_wait(met.at[k], len(rounds[k]))
+
+    everyone = n_span * n_width
+    me = s * n_width + w
+
+    def to_all(buf, ssem, rsem):
+        @pl.loop(1, everyone)
+        def _(off):
+            other = lax.rem(me + off, everyone)
+            pltpu.make_async_remote_copy(
+                src_ref=buf.at[me], dst_ref=buf.at[me], send_sem=ssem, recv_sem=rsem,
+                device_id=(other // n_width, other % n_width), device_id_type=MESH,
+            ).start()
+
+    def all_of(buf, sem):
+        others = buf.at[pl.ds(0, everyone - 1)]
+        pltpu.make_async_copy(others, others, sem).wait()
 
     def split(x):
         pairs = x.reshape(kp, 2, cy, cz)
@@ -122,7 +143,7 @@
         xs[e - 1, 0, i] = jnp.where(p, red[kp - 1], black[kp - 1])
         xs[e - 1, 1, i] = jnp.where(p, black[0], red[0])
 
-    pair_of = ions // 2
+    pair_of = ions // GROUPS
 
     def copy(e, k, g):
         own = pl.ds(g * pair_of, pair_of)
@@ -139,6 +160,16 @@
             device_id=to[k], device_id_type=MESH,
         )
 
+    def cond_copy(k):
+        if k >= 2:
+            src, dst = ysc.at[k - 2], yhc.at[k - 2]
+        else:
+            src, dst = cond_ref.at[cx - 1 if k == 0 else 0], xhc.at[k]
+        return pltpu.make_async_remote_copy(
+            src_ref=src, dst_ref=dst, send_sem=csend.at[k], recv_sem=crecv.at[k],
+            device_id=to[k], device_id_type=MESH,
+        )
+
     def send(e, g):
         for k in range(4):
             @pl.when(has[k])
@@ -159,6 +190,10 @@
                     yh[e, k - 2] = jnp.zeros(yh.shape[2:], F32)
                 else:
                     xh[e, k] = jnp.zeros(xh.shape[2:], F32)
+            if k >= 2:
+                yhc[k - 2] = jnp.zeros(yhc.shape[1:], F32)
+            else:
+                xhc[k] = jnp.zeros(xhc.shape[1:], F32)
 
     def pack_state(i, _):
         put_y(0, i, *split(state_ref[i]))
@@ -166,17 +201,38 @@
 
     loads[0].wait()
     lax.fori_loop(0, ions, pack_state, 0)
-    near = sum(g.astype(jnp.int32) for g in gets)
-    pl.semaphore_wait(barrier, near + len(far))
-    send(0, 0)
-    send(0, 1)
-    meet((0,))
-
-    for load in loads[1:]:
+    pl.semaphore_wait(barrier, greeted)
+    for g in range(GROUPS):
+        send(0, g)
+    meet(0)
+
+    loads[1].wait()
+    condp[0], condp[1] = split(cond_ref[...])
+    ysc[0] = jnp.concatenate([condp[0, :, cy - 1, :], condp[1, :, cy - 1, :]], axis=0)
+    ysc[1] = jnp.concatenate([condp[0, :, 0, :], condp[1, :, 0, :]], axis=0)
+    for k in range(4):
+        @pl.when(has[k])
+        def _():
+            cond_copy(k).start()
+    for load in loads[2:]:
         load.wait()
-    condp[0], condp[1] = split(cond_ref[...])
     coverp[0], coverp[1] = split(cover_ref[...].astype(F32))
-    cx_sum[...] = jnp.sum(cond_ref[...], axis=0)
+
+    eighth = lane % COARSEN
+
+    def pack(fields):
+        step = 1
+        while len(fields) > 1:
+            low = lane[:1] // step % 2 == 0
+            fields = [
+                jnp.where(low, u + pltpu.roll(u, cz - step, 1), v + pltpu.roll(v, step, 1))
+                for u, v in zip(fields[::2], fields[1::2])
+            ]
+            step *= 2
+        v = fields[0]
+        return jnp.concatenate(
+            [jnp.sum(v[j * COARSEN:(j + 1) * COARSEN], axis=0, keepdims=True)
+             for j in range(v.shape[0] // COARSEN)], axis=0)
 
     def local_terms(i, _):
         spread, strength = spread_ref[i], strength_ref[i]
@@ -198,8 +254,12 @@
         return 0
 
     lax.fori_loop(0, ions, local_terms, 0)
-    met_by((0,))
-    meet((1,))
+    cond_sum = jnp.sum(cond_ref[...], axis=0)
+    sums = pack([mx[i] for i in range(ions)] + [spread_ref[i] * cond_sum for i in range(ions)])
+    low_slot = eighth[:rows] < ions
+    coarse_off = pltpu.roll(sums, cz - ions, 1) / COARSEN
+    coarse_inv = 1.0 / jnp.where(low_slot, sums + 6.0 * coarse_off, 1.0)
+    ops[me] = jnp.where(low_slot, coarse_off * coarse_inv, pltpu.roll(coarse_inv, ions, 1))
 
     mine = colour_ref[0, 0].astype(F32)
 
@@ -225,18 +285,16 @@
         put_x(1, i, red, black)
         return 0
 
-    def halves(e, body):
-        for g in range(2):
-            receive(e, g)
-            lax.fori_loop(g * pair_of, (g + 1) * pair_of, body, 0, unroll=2)
-            if e < 2:
-                send(e + 1, g)
-
-    halves(0, phase_zero)
-    met_by((1,))
-    meet((2,))
-    met_by((2,))
-    meet((3,))
+    for g in range(GROUPS):
+        receive(0, g)
+        lax.fori_loop(g * pair_of, (g + 1) * pair_of, phase_zero, 0, unroll=UNROLL)
+        send(1, g)
+    met_by(0)
+    meet(1)
+    for k in range(4):
+        @pl.when(gets[k])
+        def _():
+            cond_copy(k).wait_recv()
 
     def phase_one(i, _):
         near = rim(1, i)
@@ -248,99 +306,96 @@
         d[0, i], d[1, i] = red, black
         put_y(2, i, red, black)
         put_x(2, i, red, black)
-        return 0
-
-    halves(1, phase_one)
-    met_by((3,))
-    meet((4,))
-
-    eighth = lane % COARSEN
-
-    def coarse_pack(parts):
-        acc = jnp.zeros((cy, cz), F32)
-        for i in range(ions):
-            v = parts[i]
-            for step in (1, 2, 4):
-                v = v + pltpu.roll(v, cz - step, 1)
-            if i:
-                v = pltpu.roll(v, i, 1)
-            acc = jnp.where(eighth == i, v, acc)
-        return jnp.concatenate(
-            [jnp.sum(acc[j * COARSEN:(j + 1) * COARSEN], axis=0, keepdims=True)
-             for j in range(rows)], axis=0)
-
-    cond_sum = cx_sum[...]
-    coarse_off = coarse_pack([spread_ref[i] * cond_sum for i in range(ions)]) / COARSEN
-    coarse_diag = coarse_pack([mx[i] for i in range(ions)]) + 6.0 * coarse_off
-    coarse_inv = 1.0 / jnp.where(eighth[:rows] < ions, coarse_diag, 1.0)
-
-
-    def fine_terms(i, _):
-        near = rim(2, i)
-        red, black = d[0, i], d[1, i]
-        near = (near[0] + nb_red(black), near[1] + nb_black(red))
+        near = (nb_red(black), nb_black(red))
         total = jnp.zeros((cy, cz), F32)
         for h, v in ((0, red), (1, black)):
             fine = rhs[h, i] - (diag[h, i] * v - spread_ref[i] * condp[h] * near[h])
             rhs[h, i] = fine
             total += jnp.sum(fine, axis=0)
-        fx[i] = total
+        fx[0, i] = total
+        fx[1, i] = spread_ref[i] * (xhc[1] * xs[1, 0, i])
+        fx[2, i] = spread_ref[i] * (xhc[0] * xs[1, 1, i])
+        for k in range(2):
+            face = ys[2, k, i]
+            other = jnp.concatenate([face[kp:], face[:kp]], axis=0)
+            py[k, i] = spread_ref[i] * jnp.sum(yhc[1 - k] * other, axis=0, keepdims=True)
         return 0
 
-    met_by((4,))
-    for k in range(5, len(hops)):
-        meet((k,))
-        met_by((k,))
-    halves(2, fine_terms)
-    crhs = coarse_pack([fx[i] for i in range(ions)])
-    first[w] = jnp.concatenate([crhs * coarse_inv, coarse_off * coarse_inv], axis=0)
-
-    def to_row(buf, ssem, rsem):
-        for off in range(1, n_width):
-            pltpu.make_async_remote_copy(
-                src_ref=buf.at[w], dst_ref=buf.at[w], send_sem=ssem, recv_sem=rsem,
-                device_id=(s, lax.rem(w + off, n_width)), device_id_type=MESH,
-            ).start()
-
-    def to_column(buf, ssem, rsem):
-        @pl.loop(1, n_span)
-        def _(off):
-            pltpu.make_async_remote_copy(
-                src_ref=buf.at[s], dst_ref=buf.at[s], send_sem=ssem, recv_sem=rsem,
-                device_id=(lax.rem(s + off, n_span), w), device_id_type=MESH,
-            ).start()
-
-    def all_of(buf, sem, count):
-        others = buf.at[pl.ds(0, count - 1)]
-        pltpu.make_async_copy(others, others, sem).wait()
-
-    to_row(first, gsend.at[0], grecv.at[0])
-    all_of(first, grecv.at[0], n_width)
-    gath[s] = first[...]
-    to_column(gath, gsend.at[1], grecv.at[1])
-    all_of(gath, grecv.at[1], n_span)
+    for g in range(GROUPS):
+        receive(1, g)
+        lax.fori_loop(g * pair_of, (g + 1) * pair_of, phase_one, 0, unroll=UNROLL)
+        if g == GROUPS - 2:
+            met_by(1)
+            for k in range(2, len(rounds)):
+                meet(k)
+                met_by(k)
+            to_all(ops, osend, orecv)
+
+    def column(i):
+        y_part = jnp.where(first_y, py[1, i], jnp.where(last_y, py[0, i], 0.0))
+        return (jnp.concatenate([fx[0, i], fx[2, i]], axis=0),
+                jnp.concatenate([fx[1, i], y_part], axis=0))
+
+    columns = [column(i) for i in range(ions)]
+    gath[me] = pack([u for u, _ in columns] + [v for _, v in columns])
+    to_all(gath, gsend, grecv)
+    for g in range(GROUPS):
+        send(2, g)
 
     wide = n_width * rows
-    g = gath[...]
-    aj[...] = jnp.concatenate([g[:, k, :rows] for k in range(n_width)], axis=1)
-    cj[...] = jnp.concatenate([g[:, k, rows:] for k in range(n_width)], axis=1)
+    half = n_span // 2
+    all_of(ops, orecv)
+    all_of(gath, grecv)
+
+    crow = lax.broadcasted_iota(jnp.int32, (wide, cz), 0)
+    slot_low = lax.broadcasted_iota(jnp.int32, (wide, cz), 1) % COARSEN < ions
+
+    def wide_of(v):
+        return jnp.concatenate([v[:, k] for k in range(n_width)], axis=1)
+
+    def down(v):
+        return pltpu.roll(v, cz - ions, 2)
+
+    def up(v):
+        return pltpu.roll(v, ions, 2)
+
+    def fold(low_part, high_part):
+        return jnp.where(slot_low, low_part, high_part)
+
+    plane = jnp.zeros((1, wide, cz), F32)
+    o = wide_of(ops[...].reshape(n_span, n_width, rows, cz))
+    g = gath[...].reshape(n_span, n_width, 2 * rows, cz)
+    plus, minus = wide_of(g[:, :, :rows]), wide_of(g[:, :, rows:])
+    y_sum = jnp.where(crow % rows == 0, pltpu.roll(minus, 1, 1), 0.0)
+    y_sum = jnp.where(crow % rows == rows - 1, pltpu.roll(minus, wide - 1, 1), y_sum)
+    crhs = fold(plus[:half], up(plus[half:]))
+    crhs += fold(jnp.concatenate([plane, down(plus[:half - 1])], axis=0), plus[half - 1:-1])
+    crhs += fold(minus[1:half + 1], jnp.concatenate([up(minus[half + 1:]), plane], axis=0))
+    crhs += fold(down(y_sum[:half]), y_sum[half:])
+    aj[...] = crhs * fold(down(o[:half]), o[half:])
+    cj[...] = fold(o[:half], up(o[half:]))
     crow = lax.broadcasted_iota(jnp.int32, (wide, cz), 0)
     clane = lax.broadcasted_iota(jnp.int32, (wide, cz), 1)
-    zero_c = jnp.zeros((1, wide, cz), F32)
 
     def jacobi(_, e):
-        total = jnp.concatenate([e[1:], zero_c], axis=0)
-        total += jnp.concatenate([zero_c, e[:-1]], axis=0)
+        above = jnp.where(slot_low, up_one(e[:1], -1), 0.0)
+        below = jnp.where(slot_low, 0.0, up_one(e[half - 1:], 1))
+        total = jnp.concatenate([e[1:], above], axis=0)
+        total += jnp.concatenate([below, e[:-1]], axis=0)
         total += jnp.where(crow == wide - 1, 0.0, pltpu.roll(e, wide - 1, 1))
         total += jnp.where(crow == 0, 0.0, pltpu.roll(e, 1, 1))
         total += jnp.where(clane >= cz - COARSEN, 0.0, pltpu.roll(e, cz - COARSEN, 2))
         total += jnp.where(clane < COARSEN, 0.0, pltpu.roll(e, COARSEN, 2))
         return aj[...] + cj[...] * total
 
+    def up_one(v, sign):
+        return pltpu.roll(v, ions if sign > 0 else cz - ions, 2)
+
     e = lax.fori_loop(0, COARSE_ITERS - 1, jacobi, aj[...])
-    ej[0] = zero_c[0]
-    ej[n_span + 1] = zero_c[0]
-    ej[1:n_span + 1] = e
+    ej[0] = plane[0]
+    ej[n_span + 1] = plane[0]
+    ej[1:half + 1] = e
+    ej[half + 1:n_span + 1] = down(e)
     before, here, after = ej[s], ej[s + 1], ej[s + 2]
 
     def own_rows(v):
@@ -371,8 +426,13 @@
         return jnp.concatenate(
             [jnp.broadcast_to(v[j:j + 1], (COARSEN, cz)) for j in range(rows)], axis=0)
 
+    for g in range(GROUPS):
+        receive(2, g)
     sums = []
     for i in range(ions):
+        near = rim(2, i)
+        for h in range(2):
+            rhs[h, i] += spread_ref[i] * condp[h] * near[h]
         v = sp[i]
         lift = tall(v[:rows])
         lo, hi = tall(v[rows:2 * rows]), tall(v[2 * rows:3 * rows])
@@ -395,22 +455,18 @@
                 numer += rhs[h, i, k] * im
                 denom += im * im
         sums.append((jnp.sum(numer, axis=0, keepdims=True), jnp.sum(denom, axis=0, keepdims=True)))
-    me = s * n_width + w
-    part[me] = jnp.concatenate([n for n, _ in sums] + [m for _, m in sums], axis=0)
-    everyone = n_span * n_width
-
-    @pl.loop(1, everyone)
-    def _(off):
-        other = lax.rem(me + off, everyone)
-        pltpu.make_async_remote_copy(
-            src_ref=part.at[me], dst_ref=part.at[me], send_sem=psend, recv_sem=precv,
-            device_id=(other // n_width, other % n_width), device_id_type=MESH,
-        ).start()
-
-    all_of(part, precv, everyone)
-    whole = jnp.sum(jnp.sum(part[...], axis=0), axis=1, keepdims=True)
-    weight = whole[:ions] / (whole[ions:] + EPSILON)
-    wv[...] = jnp.broadcast_to(weight, (ions, cz))
+    moments = jnp.concatenate([n for n, _ in sums] + [m for _, m in sums], axis=0)
+    moments = jnp.sum(moments, axis=1, keepdims=True)
+    share = cz // (2 * ions)
+    prow = lax.broadcasted_iota(jnp.int32, (2 * ions, cz), 0)
+    plane_of = lax.broadcasted_iota(jnp.int32, (2 * ions, cz), 1) // share
+    part[me] = jnp.sum(jnp.where(prow == plane_of, moments, 0.0), axis=0, keepdims=True)
+    to_all(part, psend, precv)
+    all_of(part, precv)
+    whole = jnp.sum(part[...], axis=0)
+    weight = whole / (pltpu.roll(whole, ions * share, 1) + EPSILON)
+    for i in range(ions):
+        wv[i:i + 1] = jnp.broadcast_to(weight[:, i * share:i * share + 1], (1, cz))
 
     for i in range(ions):
         wt = wv[i:i + 1]
@@ -428,11 +484,24 @@
         for k in range(4):
             @pl.when(has[k])
             def _():
-                copy(e, k, 0).wait_send()
-                copy(e, k, 1).wait_send()
-    all_of(first, gsend.at[0], n_width)
-    all_of(gath, gsend.at[1], n_span)
-    all_of(part, psend, everyone)
+                for g in range(GROUPS):
+                    copy(e, k, g).wait_send()
+    for k in range(4):
+        @pl.when(has[k])
+        def _():
+            cond_copy(k).wait_send()
+    all_of(ops, osend)
+    all_of(gath, gsend)
+    all_of(part, psend)
+
+
+def drain(up_ref, res_ref, up_out, res_out, sem):
+    copies = [pltpu.make_async_copy(up_ref, up_out, sem.at[0]),
+              pltpu.make_async_copy(res_ref, res_out, sem.at[1])]
+    for one in copies:
+        one.start()
+    for one in copies:
+        one.wait()
 
 
 def on_device(n_span, n_width, state, source, conductance, rebar_cover, colour, diffusivity, binding):
@@ -444,36 +513,51 @@
     vmem = pl.BlockSpec(memory_space=pltpu.VMEM)
     smem = pl.BlockSpec(memory_space=pltpu.SMEM)
     dma = pltpu.SemaphoreType.DMA
-    return pl.pallas_call(
+    anywhere = pl.BlockSpec(memory_space=pl.ANY)
+    hbm = pl.BlockSpec(memory_space=pltpu.HBM)
+    face_x = pltpu.VMEM((3, 2, ions, cy, cz), F32)
+    face_y = pltpu.VMEM((3, 2, ions, 2 * kp, cz), F32)
+    everyone = n_span * n_width
+    rounds = (n_span - 1).bit_length()
+    up, res = pl.pallas_call(
         functools.partial(kernel, n_span, n_width, ions, cx, cy, cz),
-        out_shape=(jax.ShapeDtypeStruct(state.shape, F32),) * 2,
+        out_shape=(pltpu.VMEM(state.shape, F32),) * 2,
         in_specs=[pl.BlockSpec(memory_space=pltpu.HBM)] * 4 + [smem] * 3,
         out_specs=(vmem, vmem),
         scratch_shapes=[
             pltpu.VMEM(state.shape, F32), pltpu.VMEM(state.shape, F32),
             pltpu.VMEM(conductance.shape, F32), pltpu.VMEM(conductance.shape, jnp.int32),
-            pltpu.VMEM((2, 2, ions, cy, cz), F32),
-            pltpu.VMEM((3, 2, ions, cy, cz), F32),
-            pltpu.VMEM((3, 2, ions, 2 * kp, cz), F32),
-            pltpu.VMEM((3, 2, ions, 2 * kp, cz), F32),
-            pltpu.VMEM((n_width, 2 * rows, cz), F32),
-            pltpu.VMEM((n_span, n_width, 2 * rows, cz), F32),
-            pltpu.VMEM((n_span * n_width, 2 * ions, cz), F32),
+            pltpu.VMEM((2, 2, ions, cy, cz), F32), face_x, face_y, face_y,
+            pltpu.VMEM((2, 2 * kp, cz), F32),
+            pltpu.VMEM((2, cy, cz), F32),
+            pltpu.VMEM((2, 2 * kp, cz), F32),
+            pltpu.VMEM((everyone, rows, cz), F32),
+            pltpu.VMEM((everyone, 2 * rows, cz), F32),
+            pltpu.VMEM((everyone, 1, cz), F32),
             pair, pair, half, half, half, half, half, half,
             pltpu.VMEM((ions, cy, cz), F32),
-            pltpu.VMEM((ions, cy, cz), F32),
-            pltpu.VMEM((cy, cz), F32),
-            pltpu.VMEM((n_span, n_width * rows, cz), F32),
-            pltpu.VMEM((n_span, n_width * rows, cz), F32),
+            pltpu.VMEM((3, ions, cy, cz), F32),
+            pltpu.VMEM((2, ions, 1, cz), F32),
+            pltpu.VMEM((n_span // 2, n_width * rows, cz), F32),
+            pltpu.VMEM((n_span // 2, n_width * rows, cz), F32),
             pltpu.VMEM((n_span + 2, n_width * rows, cz), F32),
             pltpu.VMEM((ions, 16, cz), F32),
             pltpu.VMEM((ions, cz), F32),
-            dma((3, 4, 2)), dma((3, 4, 2)), dma((2,)), dma((2,)), dma, dma, dma((4,)), pltpu.SemaphoreType.REGULAR((max(5, (n_span - 1).bit_length() + (n_width - 1).bit_length()),)),
+            dma((3, 4, GROUPS)), dma((3, 4, GROUPS)), dma((4,)), dma((4,)),
+            dma, dma, dma, dma, dma, dma, dma((4,)), pltpu.SemaphoreType.REGULAR((rounds,)),
         ],
         compiler_params=pltpu.CompilerParams(
-            collective_id=0, has_side_effects=True, vmem_limit_bytes=60 * 1024 * 1024
+            collective_id=0, has_side_effects=True, vmem_limit_bytes=48 * 1024 * 1024
         ),
     )(state, source, conductance, rebar_cover, colour, diffusivity, binding)
+    return pl.pallas_call(
+        drain,
+        out_shape=(jax.ShapeDtypeStruct(state.shape, F32),) * 2,
+        in_specs=[anywhere] * 2,
+        out_specs=(hbm, hbm),
+        scratch_shapes=[dma((2,))],
+        compiler_params=pltpu.CompilerParams(vmem_limit_bytes=1024 * 1024),
+    )(up, res)
 
 
 def solution(mesh):

time: 39.7 us -> 37.3 us (0.940)
  Pallas kernels: 35.5 us -> 31.8 us
  local copies, waits for them, and re-layouts: 2.72 us -> 3.89 us
    pallas_call x1, Pallas kernels: 35.5 us -> 30.9 us  [on_device(): pl.pallas_call(functools.partial(kernel, n_span, n_width, ions, cx, cy, c...]
    unnamed x4 -> x12, local copies, waits for them, and re-layouts: 2.72 us -> 3.89 us
    pallas_call x0 -> x1, Pallas kernels: none -> 0.99 us  [on_device(): pl.pallas_call(drain, out_shape=(jax.ShapeDtypeStruct(state.shape, F32),)...]
where the time goes in v1:
time: 37.3 us; the launch traced here: 37.1 us
  Pallas kernels  31.8 us (85%)
  local copies, waits for them, and re-layouts  3.89 us (10%)
  between operations  1.35 us (4%)
    pallas_call x1, Pallas kernels, on_device(): pl.pallas_call(functools.partial(kernel, n_span, n_width, ions, cx, cy, c...  30.9 us
    unnamed x12, local copies, waits for them, and re-layouts  3.89 us
    pallas_call x1, Pallas kernels, on_device(): pl.pallas_call(drain, out_shape=(jax.ShapeDtypeStruct(state.shape, F32),)...  0.99 us

profile of v1, /device:TPU:0, one launch (start us, length us, event | category | flops | bytes accessed | tf_op | source)
XLA Modules:
  0.0 37.1 jit_solution(10449184687160408160)
XLA Ops:
  0.6 0.0 copy-start.5
  0.6 0.0 copy-start.4
  1.3 0.0 copy-done.5
  1.3 0.0 copy-done.4
  1.3 0.0 copy-start
  1.3 1.0 %copy-done = f32[4,8,32,128]{3,2,1,0:T(8,128)S(1)} copy-done((f32[4,8,32,128]{3,2,1,0:T(8,128)S(1)}, f32[4,8,32,128]{3,2,1,0:T(8,128)}, u32[]{:S(2)}) %copy-start) | copy-done | bytes 524312
  2.4 0.0 copy-start.1
  2.4 1.0 %copy-done.1 = f32[4,8,32,128]{3,2,1,0:T(8,128)S(1)} copy-done((f32[4,8,32,128]{3,2,1,0:T(8,128)S(1)}, f32[4,8,32,128]{3,2,1,0:T(8,128)}, u32[]{:S(2)}) %copy-start.1) | copy-done | bytes 524312
  3.4 0.0 copy-start.2
  3.4 0.9 %copy-done.2 = f32[8,32,128]{2,1,0:T(8,128)S(1)} copy-done((f32[8,32,128]{2,1,0:T(8,128)S(1)}, f32[8,32,128]{2,1,0:T(8,128)}, u32[]{:S(2)}) %copy-start.2) | copy-done | bytes 131096
  4.3 0.0 copy-start.3
  4.3 0.9 %copy-done.3 = s32[8,32,128]{2,1,0:T(8,128)S(1)} copy-done((s32[8,32,128]{2,1,0:T(8,128)S(1)}, s32[8,32,128]{2,1,0:T(8,128)}, u32[]{:S(2)}) %copy-start.3) | copy-done | bytes 131096
  5.2 30.9 %shard_map.86 = (f32[4,8,32,128]{3,2,1,0:T(8,128)S(1)}, f32[4,8,32,128]{3,2,1,0:T(8,128)S(1)}) custom-call(f32[4,8,32,128]{3,2,1,0:T(8,128)S(1)} %copy-done, f32[4,8,32,128]{3,2,1,0:T(8,128)S(1)} %copy-done.1, f32[8,32,128]{2,1,0:T(8,128)S(1)} %copy-done.2, s32[8,32,128]{2,1,0:T(8,128)S(1)} %copy-done.3, s32[1,1]{1,0:T(1,128)S(6)} %copy.9.colour_ref, ...), custom_call_target="tpu_custom_call" | custom-call | tf_op jit(solution)/shard_map/pallas_call | solution.py:522
  36.1 1.0 %shard_map.87 = (f32[4,8,32,128]{3,2,1,0:T(8,128)}, f32[4,8,32,128]{3,2,1,0:T(8,128)}) custom-call(f32[4,8,32,128]{3,2,1,0:T(8,128)S(1)} %get-tuple-element.4.up_ref, f32[4,8,32,128]{3,2,1,0:T(8,128)S(1)} %get-tuple-element.5.res_ref), custom_call_target="tpu_custom_call" | custom-call | tf_op jit(solution)/shard_map/pallas_call | solution.py:553
Async XLA Ops:
  0.6 0.7 %copy-start.5 = (f32[4]{0:T(128)S(1)}, f32[4]{0:T(128)}, u32[]{:S(2)}) copy-start(f32[4]{0:T(128)} %strength_ref.1) | copy-start | bytes 52
  0.6 0.7 %copy-start.4 = (f32[4]{0:T(128)S(1)}, f32[4]{0:T(128)}, u32[]{:S(2)}) copy-start(f32[4]{0:T(128)} %spread_ref.1) | copy-start | bytes 52
  1.3 1.0 %copy-start = (f32[4,8,32,128]{3,2,1,0:T(8,128)S(1)}, f32[4,8,32,128]{3,2,1,0:T(8,128)}, u32[]{:S(2)}) copy-start(f32[4,8,32,128]{3,2,1,0:T(8,128)} %state_hbm.1) | copy-start | bytes 1572868
  2.4 1.0 %copy-start.1 = (f32[4,8,32,128]{3,2,1,0:T(8,128)S(1)}, f32[4,8,32,128]{3,2,1,0:T(8,128)}, u32[]{:S(2)}) copy-start(f32[4,8,32,128]{3,2,1,0:T(8,128)} %source_hbm.1) | copy-start | bytes 1572868
  3.4 0.9 %copy-start.2 = (f32[8,32,128]{2,1,0:T(8,128)S(1)}, f32[8,32,128]{2,1,0:T(8,128)}, u32[]{:S(2)}) copy-start(f32[8,32,128]{2,1,0:T(8,128)} %cond_hbm.1) | copy-start | bytes 393220
  4.3 0.9 %copy-start.3 = (s32[8,32,128]{2,1,0:T(8,128)S(1)}, s32[8,32,128]{2,1,0:T(8,128)}, u32[]{:S(2)}) copy-start(s32[8,32,128]{2,1,0:T(8,128)} %cover_hbm.1) | copy-start | bytes 393220

commit v2 on v1

--- a/solution.py
+++ b/solution.py
@@ -547,7 +547,7 @@
             dma, dma, dma, dma, dma, dma, dma((4,)), pltpu.SemaphoreType.REGULAR((rounds,)),
         ],
         compiler_params=pltpu.CompilerParams(
-            collective_id=0, has_side_effects=True, vmem_limit_bytes=48 * 1024 * 1024
+            collective_id=0, has_side_effects=True, vmem_limit_bytes=60 * 1024 * 1024
         ),
     )(state, source, conductance, rebar_cover, colour, diffusivity, binding)
     return pl.pallas_call(

time: 37.3 us -> 33 us (0.88)
  local copies, waits for them, and re-layouts: 3.89 us -> 0 us
    unnamed x12 -> x0, local copies, waits for them, and re-layouts: 3.89 us -> none
where the time goes in v2:
time: 33 us; the launch traced here: 32.9 us
  Pallas kernels  31.6 us (96%)
  between operations  1.29 us (4%)
    pallas_call x1, Pallas kernels, on_device(): pl.pallas_call(functools.partial(kernel, n_span, n_width, ions, cx, cy, c...  30.6 us
    pallas_call x1, Pallas kernels, on_device(): pl.pallas_call(drain, out_shape=(jax.ShapeDtypeStruct(state.shape, F32),)...  0.99 us

profile of v2, /device:TPU:0, one launch (start us, length us, event | category | flops | bytes accessed | tf_op | source)
XLA Modules:
  0.0 32.9 jit_solution(9037535155925729208)
XLA Ops:
  1.3 30.6 %shard_map.86 = (f32[4,8,32,128]{3,2,1,0:T(8,128)S(1)}, f32[4,8,32,128]{3,2,1,0:T(8,128)S(1)}) custom-call(f32[4,8,32,128]{3,2,1,0:T(8,128)} %state_hbm.1, f32[4,8,32,128]{3,2,1,0:T(8,128)} %source_hbm.1, f32[8,32,128]{2,1,0:T(8,128)} %cond_hbm.1, s32[8,32,128]{2,1,0:T(8,128)} %cover_hbm.1, s32[1,1]{1,0:T(1,128)S(6)} %copy.9.colour_ref, f32[4]{0:T(128)} %spread_ref.1, ...), custom_call_target="tpu_custom_call" | custom-call | tf_op jit(solution)/shard_map/pallas_call | solution.py:522
  31.9 1.0 %shard_map.87 = (f32[4,8,32,128]{3,2,1,0:T(8,128)}, f32[4,8,32,128]{3,2,1,0:T(8,128)}) custom-call(f32[4,8,32,128]{3,2,1,0:T(8,128)S(1)} %get-tuple-element.4.up_ref, f32[4,8,32,128]{3,2,1,0:T(8,128)S(1)} %get-tuple-element.5.res_ref), custom_call_target="tpu_custom_call" | custom-call | tf_op jit(solution)/shard_map/pallas_call | solution.py:553

commit v3 on v2

--- a/solution.py
+++ b/solution.py
@@ -20,10 +20,10 @@
 
 def kernel(
     n_span, n_width, ions, cx, cy, cz,
-    state_hbm, source_hbm, cond_hbm, cover_hbm, colour_ref, spread_ref, strength_ref,
+    state_hbm, source_hbm, cond_hbm, cover_hbm, colour_hbm, spread_hbm, strength_hbm,
     up_ref, res_ref,
-    state_ref, source_ref, cond_ref, cover_ref, xs, xh, ys, yh, ysc, xhc, yhc, ops, gath, part, condp, coverp, rhs, diag, c, a, d, image,
-    mx, fx, py, aj, cj, ej, sp, wv,
+    colour_ref, spread_ref, strength_ref, state_ref, source_ref, cond_ref, cover_ref, xs, xh, ys, yh, ysc, xhc, yhc, ops, gath, part, condp, coverp, rhs, diag, c, a, d, image,
+    mx, fx, aj, cj, ej, sp, wv,
     send_sem, recv_sem, csend, crecv, osend, orecv, gsend, grecv, psend, precv, in_sem, met,
 ):
     s = lax.axis_index("span")
@@ -40,7 +40,8 @@
         pltpu.make_async_copy(src, dst, in_sem.at[k])
         for k, (src, dst) in enumerate((
             (state_hbm, state_ref), (cond_hbm, cond_ref),
-            (cover_hbm, cover_ref), (source_hbm, source_ref)))
+            (cover_hbm, cover_ref), (source_hbm, source_ref),
+            (colour_hbm, colour_ref), (spread_hbm, spread_ref), (strength_hbm, strength_ref)))
     ]
     for load in loads:
         load.start()
@@ -54,34 +55,55 @@
     def flip(v, bit):
         return v + bit - 2 * bit * (v // bit % 2)
 
+    def signal(sem, moves):
+        count = 0
+        for ok, t, v in moves:
+            @pl.when(ok)
+            def _():
+                pl.semaphore_signal(sem, inc=1, device_id=(t, v), device_id_type=MESH)
+            count = count + ok.astype(jnp.int32)
+        return count
+
     quad = 4
-    high = [1 << k for k in range(2, (n_span - 1).bit_length())]
-    partners = [lax.rem(w + k, n_width) for k in range(1, n_width)]
-    quads = [s - s % quad + (s + k) % quad for k in range(1, quad)]
-    greet = [(s, v) for v in partners] + [(t, w) for t in quads] + [(flip(s, b), w) for b in high]
-    up_far = (s % quad == quad - 1) & (s < n_span - 1)
-    down_far = (s % quad == 0) & (s > 0)
-    rounds = [
-        [(s, v) for v in partners] + [(t, w) for t in quads],
-        [(flip(s, high[0]), w)] + [(flip(s, b), v) for b in high[:2] for v in partners],
-    ] + [[(flip(s, b), w)] for b in high[2:]]
-    for other in greet:
-        pl.semaphore_signal(barrier, inc=1, device_id=other, device_id_type=MESH)
-    for ok, other in ((up_far, (s + 1, w)), (down_far, (s - 1, w))):
-        @pl.when(ok)
-        def _():
-            pl.semaphore_signal(barrier, inc=1, device_id=other, device_id_type=MESH)
-    greeted = len(greet) + up_far.astype(jnp.int32) + down_far.astype(jnp.int32)
-
-    def meet(k):
-        for other in rounds[k]:
-            pl.semaphore_signal(met.at[k], inc=1, device_id=other, device_id_type=MESH)
-
-    def met_by(k):
-        pl.semaphore_wait(met.at[k], len(rounds[k]))
-
+    planes = n_span // quad
     everyone = n_span * n_width
     me = s * n_width + w
+    staged = n_width == 2 and 2 <= planes <= 4
+    if staged:
+        z = s // quad
+
+        def shifted(by):
+            return (z + by >= 0) & (z + by < planes), s + by * quad
+
+        def pairs(*moves):
+            return [shifted(by) + (v,) for by, v in moves]
+
+        always = s >= 0
+        greet = [(always, s, 1 - w), (always, flip(s, 1), w), (always, flip(s, 2), w)]
+        greet += pairs((1, w), (-1, w))
+        greet += [((s % 2 == 1) & (s < n_span - 1), s + 1, w), ((s % 2 == 0) & (s > 0), s - 1, w)]
+        rounds = [
+            [(always, s, 1 - w), (always, flip(s, 1), w)],
+            [(always, flip(s, 2), w)] + pairs((1, w), (-1, w)),
+            [(always, flip(s, 2), w)] + pairs((2, w), (-2, w), (2, 1 - w), (-2, 1 - w)),
+        ]
+        greeted = signal(barrier, greet)
+    else:
+        rounds = [[], [], []]
+        greeted = everyone - 1
+
+        @pl.loop(1, everyone)
+        def _(off):
+            other = lax.rem(me + off, everyone)
+            pl.semaphore_signal(
+                barrier, inc=1, device_id=(other // n_width, other % n_width), device_id_type=MESH)
+
+    def meet(k):
+        return signal(met.at[k], rounds[k]) if rounds[k] else 0
+
+    def met_by(k, count):
+        if rounds[k]:
+            pl.semaphore_wait(met.at[k], count)
 
     def to_all(buf, ssem, rsem):
         @pl.loop(1, everyone)
@@ -204,16 +226,12 @@
     pl.semaphore_wait(barrier, greeted)
     for g in range(GROUPS):
         send(0, g)
-    meet(0)
+    expected = meet(0)
 
     loads[1].wait()
     condp[0], condp[1] = split(cond_ref[...])
     ysc[0] = jnp.concatenate([condp[0, :, cy - 1, :], condp[1, :, cy - 1, :]], axis=0)
     ysc[1] = jnp.concatenate([condp[0, :, 0, :], condp[1, :, 0, :]], axis=0)
-    for k in range(4):
-        @pl.when(has[k])
-        def _():
-            cond_copy(k).start()
     for load in loads[2:]:
         load.wait()
     coverp[0], coverp[1] = split(cover_ref[...].astype(F32))
@@ -221,18 +239,17 @@
     eighth = lane % COARSEN
 
     def pack(fields):
-        step = 1
-        while len(fields) > 1:
-            low = lane[:1] // step % 2 == 0
-            fields = [
-                jnp.where(low, u + pltpu.roll(u, cz - step, 1), v + pltpu.roll(v, step, 1))
-                for u, v in zip(fields[::2], fields[1::2])
-            ]
-            step *= 2
-        v = fields[0]
-        return jnp.concatenate(
-            [jnp.sum(v[j * COARSEN:(j + 1) * COARSEN], axis=0, keepdims=True)
-             for j in range(v.shape[0] // COARSEN)], axis=0)
+        total = None
+        for j, v in enumerate(fields):
+            v = jnp.concatenate(
+                [jnp.sum(v[b * COARSEN:(b + 1) * COARSEN], axis=0, keepdims=True)
+                 for b in range(v.shape[0] // COARSEN)], axis=0)
+            turned = [v if l == j else pltpu.roll(v, (j - l) % cz, 1) for l in range(COARSEN)]
+            while len(turned) > 1:
+                turned = [u + t for u, t in zip(turned[::2], turned[1::2])]
+            here = eighth[:v.shape[0]] == j
+            total = turned[0] if total is None else jnp.where(here, turned[0], total)
+        return total
 
     def local_terms(i, _):
         spread, strength = spread_ref[i], strength_ref[i]
@@ -285,17 +302,18 @@
         put_x(1, i, red, black)
         return 0
 
+    met_by(0, expected)
+    expected = meet(1)
     for g in range(GROUPS):
         receive(0, g)
         lax.fori_loop(g * pair_of, (g + 1) * pair_of, phase_zero, 0, unroll=UNROLL)
         send(1, g)
-    met_by(0)
-    meet(1)
+    met_by(1, expected)
+    expected = meet(2)
     for k in range(4):
-        @pl.when(gets[k])
+        @pl.when(has[k])
         def _():
-            cond_copy(k).wait_recv()
-
+            cond_copy(k).start()
     def phase_one(i, _):
         near = rim(1, i)
         red, black = sweeps(
@@ -312,29 +330,31 @@
             fine = rhs[h, i] - (diag[h, i] * v - spread_ref[i] * condp[h] * near[h])
             rhs[h, i] = fine
             total += jnp.sum(fine, axis=0)
-        fx[0, i] = total
-        fx[1, i] = spread_ref[i] * (xhc[1] * xs[1, 0, i])
-        fx[2, i] = spread_ref[i] * (xhc[0] * xs[1, 1, i])
-        for k in range(2):
-            face = ys[2, k, i]
-            other = jnp.concatenate([face[kp:], face[:kp]], axis=0)
-            py[k, i] = spread_ref[i] * jnp.sum(yhc[1 - k] * other, axis=0, keepdims=True)
+        fx[i] = total
         return 0
 
     for g in range(GROUPS):
         receive(1, g)
+        if g == GROUPS - 1:
+            met_by(2, expected)
+            to_all(ops, osend, orecv)
         lax.fori_loop(g * pair_of, (g + 1) * pair_of, phase_one, 0, unroll=UNROLL)
-        if g == GROUPS - 2:
-            met_by(1)
-            for k in range(2, len(rounds)):
-                meet(k)
-                met_by(k)
-            to_all(ops, osend, orecv)
+
+    for k in range(4):
+        @pl.when(gets[k])
+        def _():
+            cond_copy(k).wait_recv()
+
+    def across(k, i):
+        face = ys[2, k, i]
+        other = jnp.concatenate([face[kp:], face[:kp]], axis=0)
+        return spread_ref[i] * jnp.sum(yhc[1 - k] * other, axis=0, keepdims=True)
 
     def column(i):
-        y_part = jnp.where(first_y, py[1, i], jnp.where(last_y, py[0, i], 0.0))
-        return (jnp.concatenate([fx[0, i], fx[2, i]], axis=0),
-                jnp.concatenate([fx[1, i], y_part], axis=0))
+        spread = spread_ref[i]
+        y_part = jnp.where(first_y, across(1, i), jnp.where(last_y, across(0, i), 0.0))
+        return (jnp.concatenate([fx[i], spread * (xhc[0] * xs[1, 1, i])], axis=0),
+                jnp.concatenate([spread * (xhc[1] * xs[1, 0, i]), y_part], axis=0))
 
     columns = [column(i) for i in range(ions)]
     gath[me] = pack([u for u, _ in columns] + [v for _, v in columns])
@@ -416,11 +436,10 @@
          jnp.zeros((16 - 3 * rows - 2, cz), F32)], axis=0)
     for i in range(ions):
         v = jnp.where(eighth[:16] == i, packed, 0.0)
-        if i:
-            v = pltpu.roll(v, cz - i, 1)
-        for step in (1, 2, 4):
-            v = v + pltpu.roll(v, step, 1)
-        sp[i] = v
+        turned = [v if l == i else pltpu.roll(v, (l - i) % cz, 1) for l in range(COARSEN)]
+        while len(turned) > 1:
+            turned = [u + t for u, t in zip(turned[::2], turned[1::2])]
+        sp[i] = turned[0]
 
     def tall(v):
         return jnp.concatenate(
@@ -457,14 +476,16 @@
         sums.append((jnp.sum(numer, axis=0, keepdims=True), jnp.sum(denom, axis=0, keepdims=True)))
     moments = jnp.concatenate([n for n, _ in sums] + [m for _, m in sums], axis=0)
     moments = jnp.sum(moments, axis=1, keepdims=True)
-    share = cz // (2 * ions)
-    prow = lax.broadcasted_iota(jnp.int32, (2 * ions, cz), 0)
-    plane_of = lax.broadcasted_iota(jnp.int32, (2 * ions, cz), 1) // share
-    part[me] = jnp.sum(jnp.where(prow == plane_of, moments, 0.0), axis=0, keepdims=True)
+    share = cz // ions
+    prow = lax.broadcasted_iota(jnp.int32, (ions, cz), 0)
+    mine_of = prow == lax.broadcasted_iota(jnp.int32, (ions, cz), 1) // share
+    part[me] = jnp.concatenate(
+        [jnp.sum(jnp.where(mine_of, v, 0.0), axis=0, keepdims=True)
+         for v in (moments[:ions], moments[ions:])], axis=0)
     to_all(part, psend, precv)
     all_of(part, precv)
     whole = jnp.sum(part[...], axis=0)
-    weight = whole / (pltpu.roll(whole, ions * share, 1) + EPSILON)
+    weight = whole[:1] / (whole[1:] + EPSILON)
     for i in range(ions):
         wv[i:i + 1] = jnp.broadcast_to(weight[:, i * share:i * share + 1], (1, cz))
 
@@ -511,20 +532,19 @@
     half = pltpu.VMEM((2, ions, kp, cy, cz), F32)
     pair = pltpu.VMEM((2, kp, cy, cz), F32)
     vmem = pl.BlockSpec(memory_space=pltpu.VMEM)
-    smem = pl.BlockSpec(memory_space=pltpu.SMEM)
     dma = pltpu.SemaphoreType.DMA
     anywhere = pl.BlockSpec(memory_space=pl.ANY)
     hbm = pl.BlockSpec(memory_space=pltpu.HBM)
     face_x = pltpu.VMEM((3, 2, ions, cy, cz), F32)
     face_y = pltpu.VMEM((3, 2, ions, 2 * kp, cz), F32)
     everyone = n_span * n_width
-    rounds = (n_span - 1).bit_length()
     up, res = pl.pallas_call(
         functools.partial(kernel, n_span, n_width, ions, cx, cy, cz),
         out_shape=(pltpu.VMEM(state.shape, F32),) * 2,
-        in_specs=[pl.BlockSpec(memory_space=pltpu.HBM)] * 4 + [smem] * 3,
+        in_specs=[pl.BlockSpec(memory_space=pltpu.HBM)] * 7,
         out_specs=(vmem, vmem),
         scratch_shapes=[
+            pltpu.SMEM((1, 1), jnp.int32), pltpu.SMEM((ions,), F32), pltpu.SMEM((ions,), F32),
             pltpu.VMEM(state.shape, F32), pltpu.VMEM(state.shape, F32),
             pltpu.VMEM(conductance.shape, F32), pltpu.VMEM(conductance.shape, jnp.int32),
             pltpu.VMEM((2, 2, ions, cy, cz), F32), face_x, face_y, face_y,
@@ -533,18 +553,17 @@
             pltpu.VMEM((2, 2 * kp, cz), F32),
             pltpu.VMEM((everyone, rows, cz), F32),
             pltpu.VMEM((everyone, 2 * rows, cz), F32),
-            pltpu.VMEM((everyone, 1, cz), F32),
+            pltpu.VMEM((everyone, 2, cz), F32),
             pair, pair, half, half, half, half, half, half,
             pltpu.VMEM((ions, cy, cz), F32),
-            pltpu.VMEM((3, ions, cy, cz), F32),
-            pltpu.VMEM((2, ions, 1, cz), F32),
+            pltpu.VMEM((ions, cy, cz), F32),
             pltpu.VMEM((n_span // 2, n_width * rows, cz), F32),
             pltpu.VMEM((n_span // 2, n_width * rows, cz), F32),
             pltpu.VMEM((n_span + 2, n_width * rows, cz), F32),
             pltpu.VMEM((ions, 16, cz), F32),
             pltpu.VMEM((ions, cz), F32),
             dma((3, 4, GROUPS)), dma((3, 4, GROUPS)), dma((4,)), dma((4,)),
-            dma, dma, dma, dma, dma, dma, dma((4,)), pltpu.SemaphoreType.REGULAR((rounds,)),
+            dma, dma, dma, dma, dma, dma, dma((7,)), pltpu.SemaphoreType.REGULAR((3,)),
         ],
         compiler_params=pltpu.CompilerParams(
             collective_id=0, has_side_effects=True, vmem_limit_bytes=60 * 1024 * 1024

time: 33 us -> 31.3 us (0.948)
  Pallas kernels: 31.6 us -> 29.9 us
    pallas_call x1, Pallas kernels: 30.6 us -> 28.9 us  [on_device(): pl.pallas_call(functools.partial(kernel, n_span, n_width, ions, cx, cy, c...]
where the time goes in v3:
time: 31.3 us; the launch traced here: 31.2 us
  Pallas kernels  29.9 us (96%)
  between operations  1.29 us (4%)
    pallas_call x1, Pallas kernels, on_device(): pl.pallas_call(functools.partial(kernel, n_span, n_width, ions, cx, cy, c...  28.9 us
    pallas_call x1, Pallas kernels, on_device(): pl.pallas_call(drain, out_shape=(jax.ShapeDtypeStruct(state.shape, F32),)...  0.99 us

profile of v3, /device:TPU:0, one launch (start us, length us, event | category | flops | bytes accessed | tf_op | source)
XLA Modules:
  0.0 31.2 jit_solution(10472985771810548035)
XLA Ops:
  1.3 28.9 %shard_map.86 = (f32[4,8,32,128]{3,2,1,0:T(8,128)S(1)}, f32[4,8,32,128]{3,2,1,0:T(8,128)S(1)}) custom-call(f32[4,8,32,128]{3,2,1,0:T(8,128)} %state_hbm.1, f32[4,8,32,128]{3,2,1,0:T(8,128)} %source_hbm.1, f32[8,32,128]{2,1,0:T(8,128)} %cond_hbm.1, s32[8,32,128]{2,1,0:T(8,128)} %cover_hbm.1, s32[1,1]{1,0:T(1,128)S(6)} %copy.9.colour_hbm, f32[4]{0:T(128)} %spread_hbm.1, ...), custom_call_target="tpu_custom_call" | custom-call | tf_op jit(solution)/shard_map/pallas_call | solution.py:541
  30.2 1.0 %shard_map.87 = (f32[4,8,32,128]{3,2,1,0:T(8,128)}, f32[4,8,32,128]{3,2,1,0:T(8,128)}) custom-call(f32[4,8,32,128]{3,2,1,0:T(8,128)S(1)} %get-tuple-element.4.up_ref, f32[4,8,32,128]{3,2,1,0:T(8,128)S(1)} %get-tuple-element.5.res_ref), custom_call_target="tpu_custom_call" | custom-call | tf_op jit(solution)/shard_map/pallas_call | solution.py:572

commit v4 on v3

--- a/solution.py
+++ b/solution.py
@@ -8,13 +8,14 @@
 from jax.sharding import PartitionSpec as P
 
 COARSEN = 8
+SUB = 8
 SWEEPS = 4
 COARSE_ITERS = 20
 INV_STEP = 0.05
 EPSILON = 1e-06
 MESH = pl.DeviceIdType.MESH
 GROUPS = 2
-UNROLL = 2
+UNROLL_J = 19
 F32 = jnp.float32
 
 
@@ -30,7 +31,10 @@
     w = lax.axis_index("width")
     kp = cx // 2
     rows = cy // COARSEN
-    row = lax.broadcasted_iota(jnp.int32, (cy, cz), 0)
+    nv = cy // SUB
+    spread_of = SUB // rows
+    slot = lax.broadcasted_iota(jnp.int32, (cy, cz), 0)
+    row = slot % SUB * nv + slot // SUB
     lane = lax.broadcasted_iota(jnp.int32, (cy, cz), 1)
     p = (row + lane) % 2 == 1
     first_y, last_y = row == 0, row == cy - 1
@@ -118,14 +122,25 @@
         others = buf.at[pl.ds(0, everyone - 1)]
         pltpu.make_async_copy(others, others, sem).wait()
 
-    def split(x):
-        pairs = x.reshape(kp, 2, cy, cz)
+    def rows_of(ref, *at):
+        return jnp.concatenate(
+            [ref[at + (pl.ds(v, SUB, stride=nv), slice(None))] for v in range(nv)], axis=-2)
+
+    def split(ref, *at):
+        pairs = rows_of(ref, *at, slice(None)).reshape(kp, 2, cy, cz)
         even, odd = pairs[:, 0], pairs[:, 1]
         return jnp.where(p, odd, even), jnp.where(p, even, odd)
 
+    def y_up(v):
+        edge = jnp.where(last_y[cy - SUB:], 0.0, pltpu.roll(v[..., :SUB, :], SUB - 1, v.ndim - 2))
+        return jnp.concatenate([v[..., SUB:, :], edge], axis=-2)
+
+    def y_down(v):
+        edge = jnp.where(first_y[:SUB], 0.0, pltpu.roll(v[..., cy - SUB:, :], 1, v.ndim - 2))
+        return jnp.concatenate([edge, v[..., :cy - SUB, :]], axis=-2)
+
     def yz_sum(v):
-        out = jnp.where(last_y, 0.0, pltpu.roll(v, cy - 1, v.ndim - 2))
-        out += jnp.where(first_y, 0.0, pltpu.roll(v, 1, v.ndim - 2))
+        out = y_up(v) + y_down(v)
         out += jnp.where(last_z, 0.0, pltpu.roll(v, cz - 1, v.ndim - 1))
         out += jnp.where(first_z, 0.0, pltpu.roll(v, 1, v.ndim - 1))
         return out
@@ -143,7 +158,7 @@
         return red + jnp.where(p, below, above) + yz_sum(red)
 
     def rim(e, i):
-        lo, hi = xh[e, 0, i], xh[e, 1, i]
+        lo, hi = (rows_of(xh, e, k, i) if e == 0 else xh[e, k, i] for k in range(2))
         ylo, yhi = yh[e, 0, i], yh[e, 1, i]
         mid = jnp.zeros((kp - 2, cy, cz), F32)
 
@@ -218,7 +233,7 @@
                 xhc[k] = jnp.zeros(xhc.shape[1:], F32)
 
     def pack_state(i, _):
-        put_y(0, i, *split(state_ref[i]))
+        put_y(0, i, *split(state_ref, i))
         return 0
 
     loads[0].wait()
@@ -229,21 +244,24 @@
     expected = meet(0)
 
     loads[1].wait()
-    condp[0], condp[1] = split(cond_ref[...])
+    condp[0], condp[1] = split(cond_ref)
     ysc[0] = jnp.concatenate([condp[0, :, cy - 1, :], condp[1, :, cy - 1, :]], axis=0)
     ysc[1] = jnp.concatenate([condp[0, :, 0, :], condp[1, :, 0, :]], axis=0)
     for load in loads[2:]:
         load.wait()
-    coverp[0], coverp[1] = split(cover_ref[...].astype(F32))
+    coverp[0], coverp[1] = (v.astype(F32) for v in split(cover_ref))
 
     eighth = lane % COARSEN
 
     def pack(fields):
         total = None
         for j, v in enumerate(fields):
-            v = jnp.concatenate(
-                [jnp.sum(v[b * COARSEN:(b + 1) * COARSEN], axis=0, keepdims=True)
-                 for b in range(v.shape[0] // COARSEN)], axis=0)
+            pieces = []
+            for b in range(0, v.shape[0], cy):
+                u = sum(v[b + k * SUB:b + (k + 1) * SUB] for k in range(nv))
+                pieces += [jnp.sum(u[r:r + spread_of], axis=0, keepdims=True)
+                           for r in range(0, SUB, spread_of)]
+            v = jnp.concatenate(pieces, axis=0)
             turned = [v if l == j else pltpu.roll(v, (j - l) % cz, 1) for l in range(COARSEN)]
             while len(turned) > 1:
                 turned = [u + t for u, t in zip(turned[::2], turned[1::2])]
@@ -253,8 +271,8 @@
 
     def local_terms(i, _):
         spread, strength = spread_ref[i], strength_ref[i]
-        st = split(state_ref[i])
-        src = split(source_ref[i])
+        st = split(state_ref, i)
+        src = split(source_ref, i)
         near = (nb_red(st[1]), nb_black(st[0]))
         mass_sum = jnp.zeros((cy, cz), F32)
         for h in range(2):
@@ -271,7 +289,7 @@
         return 0
 
     lax.fori_loop(0, ions, local_terms, 0)
-    cond_sum = jnp.sum(cond_ref[...], axis=0)
+    cond_sum = jnp.sum(condp[0] + condp[1], axis=0)
     sums = pack([mx[i] for i in range(ions)] + [spread_ref[i] * cond_sum for i in range(ions)])
     low_slot = eighth[:rows] < ions
     coarse_off = pltpu.roll(sums, cz - ions, 1) / COARSEN
@@ -280,33 +298,35 @@
 
     mine = colour_ref[0, 0].astype(F32)
 
-    def sweeps(ar, ab, cr, cb):
-        red = ar
-        black = ab + cb * nb_black(red)
+    def sweeps(mask, right, ids):
+        coefs = [(c[0, i], c[1, i]) for i in ids]
+        red = [mask * ar for ar, _ in right]
+        ab = [mask * v for _, v in right]
+        ar = list(red)
+        black = [v + cc[1] * nb_black(r) for v, cc, r in zip(ab, coefs, red)]
         for _ in range(SWEEPS - 1):
-            red = ar + cr * nb_red(black)
-            black = ab + cb * nb_black(red)
+            red = [v + cc[0] * nb_red(u) for v, cc, u in zip(ar, coefs, black)]
+            black = [v + cc[1] * nb_black(r) for v, cc, r in zip(ab, coefs, red)]
         return red, black
 
-    def phase_zero(i, _):
-        near = rim(0, i)
-        for h in range(2):
-            right = rhs[h, i] + spread_ref[i] * condp[h] * near[h]
-            rhs[h, i] = right
-            a[h, i] = right / diag[h, i]
-        red, black = sweeps(
-            (1.0 - mine) * a[0, i], (1.0 - mine) * a[1, i], c[0, i], c[1, i]
-        )
-        d[0, i], d[1, i] = red, black
-        put_y(1, i, red, black)
-        put_x(1, i, red, black)
-        return 0
+    def phase_zero(ids):
+        for i in ids:
+            near = rim(0, i)
+            for h in range(2):
+                right = rhs[h, i] + spread_ref[i] * condp[h] * near[h]
+                rhs[h, i] = right
+                a[h, i] = right / diag[h, i]
+        reds, blacks = sweeps(1.0 - mine, [(a[0, i], a[1, i]) for i in ids], ids)
+        for i, red, black in zip(ids, reds, blacks):
+            d[0, i], d[1, i] = red, black
+            put_y(1, i, red, black)
+            put_x(1, i, red, black)
 
     met_by(0, expected)
     expected = meet(1)
     for g in range(GROUPS):
         receive(0, g)
-        lax.fori_loop(g * pair_of, (g + 1) * pair_of, phase_zero, 0, unroll=UNROLL)
+        phase_zero(range(g * pair_of, (g + 1) * pair_of))
         send(1, g)
     met_by(1, expected)
     expected = meet(2)
@@ -314,31 +334,32 @@
         @pl.when(has[k])
         def _():
             cond_copy(k).start()
-    def phase_one(i, _):
-        near = rim(1, i)
-        red, black = sweeps(
-            mine * (a[0, i] + c[0, i] * near[0]), mine * (a[1, i] + c[1, i] * near[1]),
-            c[0, i], c[1, i],
-        )
-        red, black = red + d[0, i], black + d[1, i]
-        d[0, i], d[1, i] = red, black
-        put_y(2, i, red, black)
-        put_x(2, i, red, black)
-        near = (nb_red(black), nb_black(red))
-        total = jnp.zeros((cy, cz), F32)
-        for h, v in ((0, red), (1, black)):
-            fine = rhs[h, i] - (diag[h, i] * v - spread_ref[i] * condp[h] * near[h])
-            rhs[h, i] = fine
-            total += jnp.sum(fine, axis=0)
-        fx[i] = total
-        return 0
+    def phase_one(ids):
+        right = []
+        for i in ids:
+            near = rim(1, i)
+            right.append((a[0, i] + c[0, i] * near[0], a[1, i] + c[1, i] * near[1]))
+        reds, blacks = sweeps(mine, right, ids)
+        for i, red, black in zip(ids, reds, blacks):
+            red, black = red + d[0, i], black + d[1, i]
+            d[0, i], d[1, i] = red, black
+            put_y(2, i, red, black)
+            put_x(2, i, red, black)
+            near = (nb_red(black), nb_black(red))
+            total = jnp.zeros((cy, cz), F32)
+            for h, v in ((0, red), (1, black)):
+                fine = rhs[h, i] - (diag[h, i] * v - spread_ref[i] * condp[h] * near[h])
+                rhs[h, i] = fine
+                total += jnp.sum(fine, axis=0)
+            fx[i] = total
 
     for g in range(GROUPS):
         receive(1, g)
         if g == GROUPS - 1:
             met_by(2, expected)
             to_all(ops, osend, orecv)
-        lax.fori_loop(g * pair_of, (g + 1) * pair_of, phase_one, 0, unroll=UNROLL)
+        phase_one(range(g * pair_of, (g + 1) * pair_of))
+        send(2, g)
 
     for k in range(4):
         @pl.when(gets[k])
@@ -353,19 +374,15 @@
     def column(i):
         spread = spread_ref[i]
         y_part = jnp.where(first_y, across(1, i), jnp.where(last_y, across(0, i), 0.0))
-        return (jnp.concatenate([fx[i], spread * (xhc[0] * xs[1, 1, i])], axis=0),
-                jnp.concatenate([spread * (xhc[1] * xs[1, 0, i]), y_part], axis=0))
+        return (jnp.concatenate([fx[i], spread * (rows_of(xhc, 0) * xs[1, 1, i])], axis=0),
+                jnp.concatenate([spread * (rows_of(xhc, 1) * xs[1, 0, i]), y_part], axis=0))
 
     columns = [column(i) for i in range(ions)]
     gath[me] = pack([u for u, _ in columns] + [v for _, v in columns])
     to_all(gath, gsend, grecv)
-    for g in range(GROUPS):
-        send(2, g)
 
     wide = n_width * rows
     half = n_span // 2
-    all_of(ops, orecv)
-    all_of(gath, grecv)
 
     crow = lax.broadcasted_iota(jnp.int32, (wide, cz), 0)
     slot_low = lax.broadcasted_iota(jnp.int32, (wide, cz), 1) % COARSEN < ions
@@ -383,7 +400,20 @@
         return jnp.where(slot_low, low_part, high_part)
 
     plane = jnp.zeros((1, wide, cz), F32)
+    all_of(ops, orecv)
     o = wide_of(ops[...].reshape(n_span, n_width, rows, cz))
+    aj[...] = fold(down(o[:half]), o[half:])
+    cj[...] = fold(o[:half], up(o[half:]))
+    def face_terms(i, _):
+        near = rim(2, i)
+        for h in range(2):
+            rhs[h, i] += spread_ref[i] * condp[h] * near[h]
+        return 0
+
+    for g in range(GROUPS):
+        receive(2, g)
+    lax.fori_loop(0, ions, face_terms, 0)
+    all_of(gath, grecv)
     g = gath[...].reshape(n_span, n_width, 2 * rows, cz)
     plus, minus = wide_of(g[:, :, :rows]), wide_of(g[:, :, rows:])
     y_sum = jnp.where(crow % rows == 0, pltpu.roll(minus, 1, 1), 0.0)
@@ -392,26 +422,27 @@
     crhs += fold(jnp.concatenate([plane, down(plus[:half - 1])], axis=0), plus[half - 1:-1])
     crhs += fold(minus[1:half + 1], jnp.concatenate([up(minus[half + 1:]), plane], axis=0))
     crhs += fold(down(y_sum[:half]), y_sum[half:])
-    aj[...] = crhs * fold(down(o[:half]), o[half:])
-    cj[...] = fold(o[:half], up(o[half:]))
+    aj[...] = crhs * aj[...]
     crow = lax.broadcasted_iota(jnp.int32, (wide, cz), 0)
     clane = lax.broadcasted_iota(jnp.int32, (wide, cz), 1)
+
+    y_plus = jnp.where(crow == wide - 1, 0.0, cj[...])
+    y_minus = jnp.where(crow == 0, 0.0, cj[...])
+    z_plus = jnp.where(clane >= cz - COARSEN, 0.0, cj[...])
+    z_minus = jnp.where(clane < COARSEN, 0.0, cj[...])
 
     def jacobi(_, e):
         above = jnp.where(slot_low, up_one(e[:1], -1), 0.0)
         below = jnp.where(slot_low, 0.0, up_one(e[half - 1:], 1))
-        total = jnp.concatenate([e[1:], above], axis=0)
-        total += jnp.concatenate([below, e[:-1]], axis=0)
-        total += jnp.where(crow == wide - 1, 0.0, pltpu.roll(e, wide - 1, 1))
-        total += jnp.where(crow == 0, 0.0, pltpu.roll(e, 1, 1))
-        total += jnp.where(clane >= cz - COARSEN, 0.0, pltpu.roll(e, cz - COARSEN, 2))
-        total += jnp.where(clane < COARSEN, 0.0, pltpu.roll(e, COARSEN, 2))
-        return aj[...] + cj[...] * total
+        near = jnp.concatenate([e[1:], above], axis=0) + jnp.concatenate([below, e[:-1]], axis=0)
+        total = aj[...] + cj[...] * near
+        total += y_plus * pltpu.roll(e, wide - 1, 1) + y_minus * pltpu.roll(e, 1, 1)
+        return total + (z_plus * pltpu.roll(e, cz - COARSEN, 2) + z_minus * pltpu.roll(e, COARSEN, 2))
 
     def up_one(v, sign):
         return pltpu.roll(v, ions if sign > 0 else cz - ions, 2)
 
-    e = lax.fori_loop(0, COARSE_ITERS - 1, jacobi, aj[...])
+    e = lax.fori_loop(0, COARSE_ITERS - 1, jacobi, aj[...], unroll=UNROLL_J)
     ej[0] = plane[0]
     ej[n_span + 1] = plane[0]
     ej[1:half + 1] = e
@@ -443,15 +474,10 @@
 
     def tall(v):
         return jnp.concatenate(
-            [jnp.broadcast_to(v[j:j + 1], (COARSEN, cz)) for j in range(rows)], axis=0)
-
-    for g in range(GROUPS):
-        receive(2, g)
+            [jnp.broadcast_to(v[j:j + 1], (spread_of, cz)) for j in range(rows)] * nv, axis=0)
+
     sums = []
     for i in range(ions):
-        near = rim(2, i)
-        for h in range(2):
-            rhs[h, i] += spread_ref[i] * condp[h] * near[h]
         v = sp[i]
         lift = tall(v[:rows])
         lo, hi = tall(v[rows:2 * rows]), tall(v[2 * rows:3 * rows])
@@ -483,6 +509,24 @@
         [jnp.sum(jnp.where(mine_of, v, 0.0), axis=0, keepdims=True)
          for v in (moments[:ions], moments[ions:])], axis=0)
     to_all(part, psend, precv)
+
+    def put(ref, i, x, value, add=None):
+        for v in range(nv):
+            at = (i, x, pl.ds(v, SUB, stride=nv), slice(None))
+            piece = value[v * SUB:(v + 1) * SUB]
+            ref[at] = piece if add is None else add[at] + piece
+
+    def to_rows(i, _):
+        for k in range(kp):
+            for out, red, black, add in (
+                    (up_ref, d[0, i, k], d[1, i, k], state_ref),
+                    (res_ref, rhs[0, i, k], rhs[1, i, k], None),
+                    (source_ref, image[0, i, k], image[1, i, k], None)):
+                put(out, i, 2 * k, jnp.where(p, black, red), add)
+                put(out, i, 2 * k + 1, jnp.where(p, red, black), add)
+        return 0
+
+    lax.fori_loop(0, ions, to_rows, 0)
     all_of(part, precv)
     whole = jnp.sum(part[...], axis=0)
     weight = whole[:1] / (whole[1:] + EPSILON)
@@ -491,15 +535,10 @@
 
     for i in range(ions):
         wt = wv[i:i + 1]
-        lifted = wt * tall(sp[i, :rows])
-        for k in range(kp):
-            red, black = d[0, i, k], d[1, i, k]
-            up_ref[i, 2 * k] = state_ref[i, 2 * k] + (jnp.where(p, black, red) + lifted)
-            up_ref[i, 2 * k + 1] = state_ref[i, 2 * k + 1] + (jnp.where(p, red, black) + lifted)
-            red = rhs[0, i, k] - wt * image[0, i, k]
-            black = rhs[1, i, k] - wt * image[1, i, k]
-            res_ref[i, 2 * k] = jnp.where(p, black, red)
-            res_ref[i, 2 * k + 1] = jnp.where(p, red, black)
+        lifted = wt * jnp.concatenate(
+            [jnp.broadcast_to(sp[i, j:j + 1], (COARSEN, cz)) for j in range(rows)], axis=0)
+        up_ref[i] = up_ref[i] + lifted
+        res_ref[i] = res_ref[i] - wt * source_ref[i]
 
     for e in range(3):
         for k in range(4):

time: 31.3 us -> 30.8 us (0.984)
  Pallas kernels: 29.9 us -> 29.3 us
    pallas_call x1, Pallas kernels: 28.9 us -> 28.4 us  [on_device(): pl.pallas_call(functools.partial(kernel, n_span, n_width, ions, cx, cy, c...]
where the time goes in v4:
time: 30.8 us; the launch traced here: 30.6 us
  Pallas kernels  29.3 us (95%)
  between operations  1.29 us (4%)
    pallas_call x1, Pallas kernels, on_device(): pl.pallas_call(functools.partial(kernel, n_span, n_width, ions, cx, cy, c...  28.4 us
    pallas_call x1, Pallas kernels, on_device(): pl.pallas_call(drain, out_shape=(jax.ShapeDtypeStruct(state.shape, F32),)...  0.99 us

profile of v4, /device:TPU:0, one launch (start us, length us, event | category | flops | bytes accessed | tf_op | source)
XLA Modules:
  0.0 30.6 jit_solution(8345020087371406977)
XLA Ops:
  1.3 28.4 %shard_map.86 = (f32[4,8,32,128]{3,2,1,0:T(8,128)S(1)}, f32[4,8,32,128]{3,2,1,0:T(8,128)S(1)}) custom-call(f32[4,8,32,128]{3,2,1,0:T(8,128)} %state_hbm.1, f32[4,8,32,128]{3,2,1,0:T(8,128)} %source_hbm.1, f32[8,32,128]{2,1,0:T(8,128)} %cond_hbm.1, s32[8,32,128]{2,1,0:T(8,128)} %cover_hbm.1, s32[1,1]{1,0:T(1,128)S(6)} %copy.9.colour_hbm, f32[4]{0:T(128)} %spread_hbm.1, ...), custom_call_target="tpu_custom_call" | custom-call | tf_op jit(solution)/shard_map/pallas_call | solution.py:580
  29.6 1.0 %shard_map.87 = (f32[4,8,32,128]{3,2,1,0:T(8,128)}, f32[4,8,32,128]{3,2,1,0:T(8,128)}) custom-call(f32[4,8,32,128]{3,2,1,0:T(8,128)S(1)} %get-tuple-element.4.up_ref, f32[4,8,32,128]{3,2,1,0:T(8,128)S(1)} %get-tuple-element.5.res_ref), custom_call_target="tpu_custom_call" | custom-call | tf_op jit(solution)/shard_map/pallas_call | solution.py:611

commit v5 on v4

--- a/solution.py
+++ b/solution.py
@@ -72,6 +72,7 @@
     planes = n_span // quad
     everyone = n_span * n_width
     me = s * n_width + w
+    partners = [lax.rem(w + k, n_width) for k in range(1, n_width)]
     staged = n_width == 2 and 2 <= planes <= 4
     if staged:
         z = s // quad
@@ -109,14 +110,52 @@
         if rounds[k]:
             pl.semaphore_wait(met.at[k], count)
 
+    def bits_of(v, count):
+        return [((v // b % 2) * b, b - (v // b % 2) * b) for b in (1 << k for k in range(count))]
+
+    def far(off):
+        at = off // n_width
+        return at // quad + at % quad // 2 + at % 2
+
+    span_bits, width_bits = (n_span - 1).bit_length(), (n_width - 1).bit_length()
+    listed = everyone == 1 << (span_bits + width_bits) and everyone <= 64
+    span_of, width_of = bits_of(s, span_bits), bits_of(w, width_bits)
+
     def to_all(buf, ssem, rsem):
-        @pl.loop(1, everyone)
-        def _(off):
-            other = lax.rem(me + off, everyone)
+        def send_to(t, v):
             pltpu.make_async_remote_copy(
                 src_ref=buf.at[me], dst_ref=buf.at[me], send_sem=ssem, recv_sem=rsem,
-                device_id=(other // n_width, other % n_width), device_id_type=MESH,
+                device_id=(t, v), device_id_type=MESH,
             ).start()
+
+        if listed:
+            for off in sorted(range(1, everyone), key=far, reverse=True):
+                at_s, at_w = off // n_width, off % n_width
+                send_to(sum(pair[at_s >> k & 1] for k, pair in enumerate(span_of)),
+                        sum(pair[at_w >> k & 1] for k, pair in enumerate(width_of)))
+        else:
+            @pl.loop(1, everyone)
+            def _(off):
+                other = lax.rem(me + off, everyone)
+                send_to(other // n_width, other % n_width)
+
+    def ops_along(first, last):
+        for off in sorted(range(first, last), key=lambda k: far(k * n_width), reverse=True):
+            t = sum(pair[off >> k & 1] for k, pair in enumerate(span_of)) if listed else lax.rem(s + off, n_span)
+            pltpu.make_async_remote_copy(
+                src_ref=ops.at[w, s], dst_ref=ops.at[w, s], send_sem=osend.at[0], recv_sem=orecv.at[0],
+                device_id=(t, w), device_id_type=MESH,
+            ).start()
+
+    def ops_across(k):
+        return pltpu.make_async_remote_copy(
+            src_ref=ops.at[w], dst_ref=ops.at[w], send_sem=osend.at[k], recv_sem=orecv.at[k],
+            device_id=(s, partners[k - 1]), device_id_type=MESH,
+        )
+
+    def ops_column(sem):
+        others = ops.at[w, pl.ds(0, n_span - 1)]
+        pltpu.make_async_copy(others, others, sem).wait()
 
     def all_of(buf, sem):
         others = buf.at[pl.ds(0, everyone - 1)]
@@ -283,7 +322,7 @@
             dg = mass + 6.0 * coef
             diag[h, i] = dg
             c[h, i] = coef / dg
-            rhs[h, i] = src[h] - (coef * (6.0 * st[h] - near[h]) + bound * st[h])
+            a[h, i] = (src[h] - (coef * (6.0 * st[h] - near[h]) + bound * st[h])) / dg
             mass_sum += jnp.sum(mass, axis=0)
         mx[i] = mass_sum
         return 0
@@ -294,7 +333,7 @@
     low_slot = eighth[:rows] < ions
     coarse_off = pltpu.roll(sums, cz - ions, 1) / COARSEN
     coarse_inv = 1.0 / jnp.where(low_slot, sums + 6.0 * coarse_off, 1.0)
-    ops[me] = jnp.where(low_slot, coarse_off * coarse_inv, pltpu.roll(coarse_inv, ions, 1))
+    ops[w, s] = jnp.where(low_slot, coarse_off * coarse_inv, pltpu.roll(coarse_inv, ions, 1))
 
     mine = colour_ref[0, 0].astype(F32)
 
@@ -313,9 +352,7 @@
         for i in ids:
             near = rim(0, i)
             for h in range(2):
-                right = rhs[h, i] + spread_ref[i] * condp[h] * near[h]
-                rhs[h, i] = right
-                a[h, i] = right / diag[h, i]
+                a[h, i] = a[h, i] + c[h, i] * near[h]
         reds, blacks = sweeps(1.0 - mine, [(a[0, i], a[1, i]) for i in ids], ids)
         for i, red, black in zip(ids, reds, blacks):
             d[0, i], d[1, i] = red, black
@@ -345,19 +382,17 @@
             d[0, i], d[1, i] = red, black
             put_y(2, i, red, black)
             put_x(2, i, red, black)
-            near = (nb_red(black), nb_black(red))
-            total = jnp.zeros((cy, cz), F32)
-            for h, v in ((0, red), (1, black)):
-                fine = rhs[h, i] - (diag[h, i] * v - spread_ref[i] * condp[h] * near[h])
-                rhs[h, i] = fine
-                total += jnp.sum(fine, axis=0)
-            fx[i] = total
+            fine = diag[0, i] * (a[0, i] + c[0, i] * nb_red(black) - red)
+            rhs[0, i] = fine
+            still = -mine * (spread_ref[i] * condp[1] * rim(1, i)[1])
+            rhs[1, i] = still
+            fx[i] = jnp.sum(fine + still, axis=0)
 
     for g in range(GROUPS):
         receive(1, g)
         if g == GROUPS - 1:
             met_by(2, expected)
-            to_all(ops, osend, orecv)
+            ops_along(1, n_span)
         phase_one(range(g * pair_of, (g + 1) * pair_of))
         send(2, g)
 
@@ -380,6 +415,9 @@
     columns = [column(i) for i in range(ions)]
     gath[me] = pack([u for u, _ in columns] + [v for _, v in columns])
     to_all(gath, gsend, grecv)
+    ops_column(orecv.at[0])
+    for k in range(1, n_width):
+        ops_across(k).start()
 
     wide = n_width * rows
     half = n_span // 2
@@ -400,8 +438,9 @@
         return jnp.where(slot_low, low_part, high_part)
 
     plane = jnp.zeros((1, wide, cz), F32)
-    all_of(ops, orecv)
-    o = wide_of(ops[...].reshape(n_span, n_width, rows, cz))
+    for k in range(1, n_width):
+        ops_across(k).wait_recv()
+    o = jnp.concatenate([ops[k] for k in range(n_width)], axis=1)
     aj[...] = fold(down(o[:half]), o[half:])
     cj[...] = fold(o[:half], up(o[half:]))
     def face_terms(i, _):
@@ -550,7 +589,9 @@
         @pl.when(has[k])
         def _():
             cond_copy(k).wait_send()
-    all_of(ops, osend)
+    ops_column(osend.at[0])
+    for k in range(1, n_width):
+        ops_across(k).wait_send()
     all_of(gath, gsend)
     all_of(part, psend)
 
@@ -590,7 +631,7 @@
             pltpu.VMEM((2, 2 * kp, cz), F32),
             pltpu.VMEM((2, cy, cz), F32),
             pltpu.VMEM((2, 2 * kp, cz), F32),
-            pltpu.VMEM((everyone, rows, cz), F32),
+            pltpu.VMEM((n_width, n_span, rows, cz), F32),
             pltpu.VMEM((everyone, 2 * rows, cz), F32),
             pltpu.VMEM((everyone, 2, cz), F32),
             pair, pair, half, half, half, half, half, half,
@@ -602,7 +643,7 @@
             pltpu.VMEM((ions, 16, cz), F32),
             pltpu.VMEM((ions, cz), F32),
             dma((3, 4, GROUPS)), dma((3, 4, GROUPS)), dma((4,)), dma((4,)),
-            dma, dma, dma, dma, dma, dma, dma((7,)), pltpu.SemaphoreType.REGULAR((3,)),
+            dma((n_width,)), dma((n_width,)), dma, dma, dma, dma, dma((7,)), pltpu.SemaphoreType.REGULAR((3,)),
         ],
         compiler_params=pltpu.CompilerParams(
             collective_id=0, has_side_effects=True, vmem_limit_bytes=60 * 1024 * 1024

time: 30.8 us -> 30.2 us (0.981)
  Pallas kernels: 29.3 us -> 28.8 us
    pallas_call x1, Pallas kernels: 28.4 us -> 27.8 us  [on_device(): pl.pallas_call(functools.partial(kernel, n_span, n_width, ions, cx, cy, c...]
where the time goes in v5:
time: 30.2 us; the launch traced here: 30.1 us
  Pallas kernels  28.8 us (95%)
  between operations  1.29 us (4%)
    pallas_call x1, Pallas kernels, on_device(): pl.pallas_call(functools.partial(kernel, n_span, n_width, ions, cx, cy, c...  27.8 us
    pallas_call x1, Pallas kernels, on_device(): pl.pallas_call(drain, out_shape=(jax.ShapeDtypeStruct(state.shape, F32),)...  0.99 us

profile of v5, /device:TPU:0, one launch (start us, length us, event | category | flops | bytes accessed | tf_op | source)
XLA Modules:
  0.0 30.1 jit_solution(11954891540397137384)
XLA Ops:
  1.3 27.8 %shard_map.86 = (f32[4,8,32,128]{3,2,1,0:T(8,128)S(1)}, f32[4,8,32,128]{3,2,1,0:T(8,128)S(1)}) custom-call(f32[4,8,32,128]{3,2,1,0:T(8,128)} %state_hbm.1, f32[4,8,32,128]{3,2,1,0:T(8,128)} %source_hbm.1, f32[8,32,128]{2,1,0:T(8,128)} %cond_hbm.1, s32[8,32,128]{2,1,0:T(8,128)} %cover_hbm.1, s32[1,1]{1,0:T(1,128)S(6)} %copy.9.colour_hbm, f32[4]{0:T(128)} %spread_hbm.1, ...), custom_call_target="tpu_custom_call" | custom-call | tf_op jit(solution)/shard_map/pallas_call | solution.py:621
  29.1 1.0 %shard_map.87 = (f32[4,8,32,128]{3,2,1,0:T(8,128)}, f32[4,8,32,128]{3,2,1,0:T(8,128)}) custom-call(f32[4,8,32,128]{3,2,1,0:T(8,128)S(1)} %get-tuple-element.4.up_ref, f32[4,8,32,128]{3,2,1,0:T(8,128)S(1)} %get-tuple-element.5.res_ref), custom_call_target="tpu_custom_call" | custom-call | tf_op jit(solution)/shard_map/pallas_call | solution.py:652

commit v6 on v5

--- a/solution.py
+++ b/solution.py
@@ -394,7 +394,6 @@
             met_by(2, expected)
             ops_along(1, n_span)
         phase_one(range(g * pair_of, (g + 1) * pair_of))
-        send(2, g)
 
     for k in range(4):
         @pl.when(gets[k])
@@ -415,6 +414,8 @@
     columns = [column(i) for i in range(ions)]
     gath[me] = pack([u for u, _ in columns] + [v for _, v in columns])
     to_all(gath, gsend, grecv)
+    for g in range(GROUPS):
+        send(2, g)
     ops_column(orecv.at[0])
     for k in range(1, n_width):
         ops_across(k).start()
@@ -443,15 +444,6 @@
     o = jnp.concatenate([ops[k] for k in range(n_width)], axis=1)
     aj[...] = fold(down(o[:half]), o[half:])
     cj[...] = fold(o[:half], up(o[half:]))
-    def face_terms(i, _):
-        near = rim(2, i)
-        for h in range(2):
-            rhs[h, i] += spread_ref[i] * condp[h] * near[h]
-        return 0
-
-    for g in range(GROUPS):
-        receive(2, g)
-    lax.fori_loop(0, ions, face_terms, 0)
     all_of(gath, grecv)
     g = gath[...].reshape(n_span, n_width, 2 * rows, cz)
     plus, minus = wide_of(g[:, :, :rows]), wide_of(g[:, :, rows:])
@@ -486,6 +478,15 @@
     ej[n_span + 1] = plane[0]
     ej[1:half + 1] = e
     ej[half + 1:n_span + 1] = down(e)
+    def face_terms(i, _):
+        near = rim(2, i)
+        for h in range(2):
+            rhs[h, i] += spread_ref[i] * condp[h] * near[h]
+        return 0
+
+    for g in range(GROUPS):
+        receive(2, g)
+    lax.fori_loop(0, ions, face_terms, 0)
     before, here, after = ej[s], ej[s + 1], ej[s + 2]
 
     def own_rows(v):

time: 30.2 us -> 29.7 us (0.983)
  Pallas kernels: 28.8 us -> 28.2 us
    pallas_call x1, Pallas kernels: 27.8 us -> 27.2 us  [on_device(): pl.pallas_call(functools.partial(kernel, n_span, n_width, ions, cx, cy, c...]
where the time goes in v6:
time: 29.7 us; the launch traced here: 29.5 us
  Pallas kernels  28.2 us (95%)
  between operations  1.29 us (4%)
    pallas_call x1, Pallas kernels, on_device(): pl.pallas_call(functools.partial(kernel, n_span, n_width, ions, cx, cy, c...  27.2 us
    pallas_call x1, Pallas kernels, on_device(): pl.pallas_call(drain, out_shape=(jax.ShapeDtypeStruct(state.shape, F32),)...  0.99 us

profile of v6, /device:TPU:0, one launch (start us, length us, event | category | flops | bytes accessed | tf_op | source)
XLA Modules:
  0.0 29.5 jit_solution(12881708474894977652)
XLA Ops:
  1.3 27.2 %shard_map.86 = (f32[4,8,32,128]{3,2,1,0:T(8,128)S(1)}, f32[4,8,32,128]{3,2,1,0:T(8,128)S(1)}) custom-call(f32[4,8,32,128]{3,2,1,0:T(8,128)} %state_hbm.1, f32[4,8,32,128]{3,2,1,0:T(8,128)} %source_hbm.1, f32[8,32,128]{2,1,0:T(8,128)} %cond_hbm.1, s32[8,32,128]{2,1,0:T(8,128)} %cover_hbm.1, s32[1,1]{1,0:T(1,128)S(6)} %copy.9.colour_hbm, f32[4]{0:T(128)} %spread_hbm.1, ...), custom_call_target="tpu_custom_call" | custom-call | tf_op jit(solution)/shard_map/pallas_call | solution.py:622
  28.5 1.0 %shard_map.87 = (f32[4,8,32,128]{3,2,1,0:T(8,128)}, f32[4,8,32,128]{3,2,1,0:T(8,128)}) custom-call(f32[4,8,32,128]{3,2,1,0:T(8,128)S(1)} %get-tuple-element.4.up_ref, f32[4,8,32,128]{3,2,1,0:T(8,128)S(1)} %get-tuple-element.5.res_ref), custom_call_target="tpu_custom_call" | custom-call | tf_op jit(solution)/shard_map/pallas_call | solution.py:653

commit v7 on v6

--- a/solution.py
+++ b/solution.py
@@ -178,23 +178,24 @@
         edge = jnp.where(first_y[:SUB], 0.0, pltpu.roll(v[..., cy - SUB:, :], 1, v.ndim - 2))
         return jnp.concatenate([edge, v[..., :cy - SUB, :]], axis=-2)
 
+    def z_sum(v):
+        return (jnp.where(last_z, 0.0, pltpu.roll(v, cz - 1, v.ndim - 1))
+                + jnp.where(first_z, 0.0, pltpu.roll(v, 1, v.ndim - 1)))
+
     def yz_sum(v):
-        out = y_up(v) + y_down(v)
-        out += jnp.where(last_z, 0.0, pltpu.roll(v, cz - 1, v.ndim - 1))
-        out += jnp.where(first_z, 0.0, pltpu.roll(v, 1, v.ndim - 1))
-        return out
+        return (y_up(v) + y_down(v)) + z_sum(v)
 
     zero_face = jnp.zeros((1, cy, cz), F32)
 
     def nb_red(black):
         above = jnp.concatenate([black[1:], zero_face], axis=0)
         below = jnp.concatenate([zero_face, black[:-1]], axis=0)
-        return black + jnp.where(p, above, below) + yz_sum(black)
+        return (black + jnp.where(p, above, below) + (y_up(black) + y_down(black))) + z_sum(black)
 
     def nb_black(red):
         above = jnp.concatenate([red[1:], zero_face], axis=0)
         below = jnp.concatenate([zero_face, red[:-1]], axis=0)
-        return red + jnp.where(p, below, above) + yz_sum(red)
+        return (red + jnp.where(p, below, above) + (y_up(red) + y_down(red))) + z_sum(red)
 
     def rim(e, i):
         lo, hi = (rows_of(xh, e, k, i) if e == 0 else xh[e, k, i] for k in range(2))
@@ -567,19 +568,6 @@
         return 0
 
     lax.fori_loop(0, ions, to_rows, 0)
-    all_of(part, precv)
-    whole = jnp.sum(part[...], axis=0)
-    weight = whole[:1] / (whole[1:] + EPSILON)
-    for i in range(ions):
-        wv[i:i + 1] = jnp.broadcast_to(weight[:, i * share:i * share + 1], (1, cz))
-
-    for i in range(ions):
-        wt = wv[i:i + 1]
-        lifted = wt * jnp.concatenate(
-            [jnp.broadcast_to(sp[i, j:j + 1], (COARSEN, cz)) for j in range(rows)], axis=0)
-        up_ref[i] = up_ref[i] + lifted
-        res_ref[i] = res_ref[i] - wt * source_ref[i]
-
     for e in range(3):
         for k in range(4):
             @pl.when(has[k])
@@ -594,6 +582,19 @@
     for k in range(1, n_width):
         ops_across(k).wait_send()
     all_of(gath, gsend)
+    all_of(part, precv)
+    whole = jnp.sum(part[...], axis=0)
+    weight = whole[:1] / (whole[1:] + EPSILON)
+    for i in range(ions):
+        wv[i:i + 1] = jnp.broadcast_to(weight[:, i * share:i * share + 1], (1, cz))
+
+    for i in range(ions):
+        wt = wv[i:i + 1]
+        lifted = wt * jnp.concatenate(
+            [jnp.broadcast_to(sp[i, j:j + 1], (COARSEN, cz)) for j in range(rows)], axis=0)
+        up_ref[i] = up_ref[i] + lifted
+        res_ref[i] = res_ref[i] - wt * source_ref[i]
+
     all_of(part, psend)
 
 

time: 29.7 us -> 29.6 us (level)
  no operation moved by 1% of the time
where the time goes in v7:
time: 29.6 us; the launch traced here: 29.5 us
  Pallas kernels  28.2 us (95%)
  between operations  1.29 us (4%)
    pallas_call x1, Pallas kernels, on_device(): pl.pallas_call(functools.partial(kernel, n_span, n_width, ions, cx, cy, c...  27.2 us
    pallas_call x1, Pallas kernels, on_device(): pl.pallas_call(drain, out_shape=(jax.ShapeDtypeStruct(state.shape, F32),)...  0.99 us

profile of v7, /device:TPU:0, one launch (start us, length us, event | category | flops | bytes accessed | tf_op | source)
XLA Modules:
  0.0 29.5 jit_solution(8493866334738742333)
XLA Ops:
  1.3 27.2 %shard_map.86 = (f32[4,8,32,128]{3,2,1,0:T(8,128)S(1)}, f32[4,8,32,128]{3,2,1,0:T(8,128)S(1)}) custom-call(f32[4,8,32,128]{3,2,1,0:T(8,128)} %state_hbm.1, f32[4,8,32,128]{3,2,1,0:T(8,128)} %source_hbm.1, f32[8,32,128]{2,1,0:T(8,128)} %cond_hbm.1, s32[8,32,128]{2,1,0:T(8,128)} %cover_hbm.1, s32[1,1]{1,0:T(1,128)S(6)} %copy.9.colour_hbm, f32[4]{0:T(128)} %spread_hbm.1, ...), custom_call_target="tpu_custom_call" | custom-call | tf_op jit(solution)/shard_map/pallas_call | solution.py:623
  28.5 1.0 %shard_map.87 = (f32[4,8,32,128]{3,2,1,0:T(8,128)}, f32[4,8,32,128]{3,2,1,0:T(8,128)}) custom-call(f32[4,8,32,128]{3,2,1,0:T(8,128)S(1)} %get-tuple-element.4.up_ref, f32[4,8,32,128]{3,2,1,0:T(8,128)S(1)} %get-tuple-element.5.res_ref), custom_call_target="tpu_custom_call" | custom-call | tf_op jit(solution)/shard_map/pallas_call | solution.py:654
